TPU v7x, 32 devices: a whole 2x2x4 slice. The times are simulated.
32 devices in a mesh: gx: 4 (over y, x), gy: 2 (over core), gz: 4 (over z).
Axes of the slice: x: 2, y: 2, z: 4, core: 2. Of those that a mesh axis runs over, the one named last changes fastest.
Arguments:
- fields: float32 [8, 96, 48, 1536], P(None, 'gx', 'gy', 'gz'), may hold values from -6 to 6
- new_owner: int32 [4, 2, 64], P('gx', 'gy', 'gz'), may hold values from 0 to 15, as said below
- new_slot: int32 [4, 2, 64], P('gx', 'gy', 'gz'), may hold values from 0 to 15, as said below
Outputs:
- indicator: float32 [96, 48, 1536], P('gx', 'gy', 'gz')
- new_blocks: float32 [4, 2, 64, 8, 20736], P('gx', 'gy', 'gz')
Inputs may be any that keep to these rules, and one draw needn't show every extreme that they name: `new_owner`: the 16 old blocks of one device go to owners among the 16 devices of its gy index, exactly 1 of them to each owner. `new_slot`: the blocks that one owner receives have distinct slots.
All inputs are finite; a program needn't handle non-finite values.
Results may differ from a plain program's by a relative error of at most 0.00007.
Values sent between devices are 32-bit elements; how exact they have to be, the bound alone decides.
No kernel may reach another device: no remote copies, remote signals or barrier semaphores. Data moves between devices by JAX's collectives and lax.ppermute only.
A program may use at most 512 MiB of HBM per device.

v0:
```python
import jax
import jax.numpy as jnp
from jax import lax
from jax.sharding import PartitionSpec as P

BS = 24


filter_weight = 0.01
base_term = 0.1


def with_halo(value, sides, width):
    for axis, dim in sides:
        size, length = (lax.axis_size(axis), value.shape[dim])
        up = [(i, (i + 1) % size) for i in range(size)]
        down = [(j, i) for i, j in up]
        last = lax.slice_in_dim(value, length - width, length, axis=dim)
        initial = lax.slice_in_dim(value, 0, width, axis=dim)
        before = lax.ppermute(last, axis, up)
        after = lax.ppermute(initial, axis, down)
        value = jnp.concatenate([before, value, after], axis=dim)
    return value


def axis_terms(lower, center, upper):
    ahead = (upper - center) * 0.5
    behind = (center - lower) * 0.5
    second = (ahead - behind) * 0.5
    spread = (
        jnp.abs(ahead)
        + jnp.abs(behind)
        + filter_weight * (jnp.abs(upper) + 2.0 * jnp.abs(center) + jnp.abs(lower))
        + base_term
    )
    return (second * second, spread * spread)


def per_device(fields, new_owner, new_slot):
    count_f = fields.shape[0]
    side_x = fields.shape[1]
    side_y = fields.shape[2]
    depth = fields.shape[3]
    block_count = depth // BS
    padded = with_halo(fields, (("gx", 1), ("gy", 2), ("gz", 3)), 2)
    center = padded[:, 2:-2, 2:-2, 2:-2]
    num_x, den_x = axis_terms(padded[:, :-4, 2:-2, 2:-2], center, padded[:, 4:, 2:-2, 2:-2])
    num_y, den_y = axis_terms(padded[:, 2:-2, :-4, 2:-2], center, padded[:, 2:-2, 4:, 2:-2])
    num_z, den_z = axis_terms(padded[:, 2:-2, 2:-2, :-4], center, padded[:, 2:-2, 2:-2, 4:])
    indicator = jnp.max(jnp.sqrt((num_x + num_y + num_z) / (den_x + den_y + den_z)), axis=0)
    wide_x = side_x + 4
    wide_y = side_y + 4
    core = padded[:, :, :, 2 : 2 + depth].reshape(count_f, wide_x, wide_y, block_count, BS)
    lower_z = padded[:, :, :, 0:depth].reshape(count_f, wide_x, wide_y, block_count, BS)[..., 0:2]
    upper_z = padded[:, :, :, 4 : 4 + depth].reshape(count_f, wide_x, wide_y, block_count, BS)[
        ..., BS - 2 : BS
    ]
    window = jnp.concatenate([lower_z, core, upper_z], axis=4).transpose(3, 0, 1, 2, 4)
    pieces = [
        window[:, :, 2:-2, 2:-2, 2:-2],
        window[:, :, 0:2, 2:-2, 2:-2],
        window[:, :, -2:, 2:-2, 2:-2],
        window[:, :, 2:-2, 0:2, 2:-2],
        window[:, :, 2:-2, -2:, 2:-2],
        window[:, :, 2:-2, 2:-2, 0:2],
        window[:, :, 2:-2, 2:-2, -2:],
    ]
    records = jnp.concatenate([piece.reshape(block_count, count_f, -1) for piece in pieces], axis=2)
    record_len = records.shape[2]
    width_x = lax.axis_size("gx")
    group_size = width_x * lax.axis_size("gz")
    capacity = block_count // group_size
    slots_total = group_size * capacity
    owners = new_owner.reshape(block_count)
    slot_ids = new_slot.reshape(block_count)
    position = jnp.arange(block_count)
    copies = jnp.sum(
        (owners[:, None] == owners[None, :]) & (position[None, :] < position[:, None]), axis=1
    )
    targets = owners * capacity + copies
    slot_range = jnp.arange(slots_total, dtype=jnp.int32)
    send_match = targets[:, None] == slot_range[None, :]
    send_table = send_match.astype(jnp.float32)
    outgoing = jnp.einsum(
        "bs,bv->sv",
        send_table,
        records.reshape(block_count, count_f * record_len),
        precision=lax.Precision.HIGHEST,
    ).reshape(slots_total, count_f, record_len)
    labels = jnp.sum(jnp.where(send_match, slot_ids[:, None], 0), axis=0)
    arrived, places = (
        lax.all_to_all(
            lax.all_to_all(
                outgoing.reshape(width_x, slots_total // width_x, count_f, record_len),
                "gx",
                split_axis=0,
                concat_axis=0,
                tiled=True,
            ),
            "gz",
            split_axis=1,
            concat_axis=1,
            tiled=True,
        ),
        lax.all_to_all(
            lax.all_to_all(
                labels.reshape(width_x, slots_total // width_x),
                "gx",
                split_axis=0,
                concat_axis=0,
                tiled=True,
            ),
            "gz",
            split_axis=1,
            concat_axis=1,
            tiled=True,
        ),
    )
    arrived = arrived.reshape(slots_total, count_f, record_len)
    places = places.reshape(slots_total)
    place_table = (places[:, None] == slot_range[None, :]).astype(jnp.float32)
    placed = jnp.einsum(
        "ps,pv->sv",
        place_table,
        arrived.reshape(slots_total, count_f * record_len),
        precision=lax.Precision.HIGHEST,
    )
    return (indicator, placed.reshape(1, 1, slots_total, count_f, record_len))


def solution(mesh):
    placed = (P(None, "gx", "gy", "gz"), P("gx", "gy", "gz"), P("gx", "gy", "gz"))
    return jax.shard_map(
        per_device,
        mesh=mesh,
        in_specs=placed,
        out_specs=(P("gx", "gy", "gz"), P("gx", "gy", "gz", None, None)),
        check_vma=False,
    )
```

profile of v0, /device:TPU:0, one launch (start us, length us, event | category | flops | bytes accessed | tf_op | source)
XLA Modules:
  0.0 1028.9 jit_solution(7950814175069603824)
XLA Ops:
  0.6 7.3 copy.56
  8.0 3.0 collective-permute-start.1
  12.0 14.1 %collective-permute-done.1 = f32[8,2,24,384]{3,0,2,1:T(8,128)S(1)} collective-permute-done((f32[8,2,24,384]{3,0,2,1:T(8,128)S(1)}, f32[8,2,24,384]{3,0,2,1:T(8,128)S(1)}, u32[]{:S(2)}, u32[]{:S(2)}) %collective-permute-start.1) | collective-permute-done | bytes 589856 | tf_op jit(solution)/shard_map/ppermute | solution.py:20
  27.0 4.6 constant_dynamic-update-slice_fusion.1
  31.6 6.6 collective-permute-done
  38.2 3.3 copy-done
  43.6 3.9 all-to-all-start
  49.3 8.4 pad_maximum_fusion.1
  57.7 5.7 fusion.30
  63.4 3.6 copy.64
  73.1 36.5 %reshape.85 = f32[8,28,28,16,24]{4,3,0,2,1:T(8,128)} reshape(f32[8,28,28,384]{3,0,2,1:T(8,128)} %pad_maximum_fusion.1) | data formatting | bytes 19267584 | tf_op jit(solution)/shard_map/reshape | solution.py:53
  109.6 2.5 copy.65
  112.2 3.6 copy.68
  115.8 18.6 %pad_maximum_fusion = (f32[8,28,28,386]{3,0,2,1:T(8,128)}, f32[8,28,28,386]{3,0,2,1:T(8,128)}) fusion(f32[8,28,28,2]{3,0,2,1:T(8,128)S(1)} %copy.65, f32[8,28,2,384]{3,0,2,1:T(8,128)} %copy-done.5, f32[8,28,24,384]{3,0,2,1:T(8,128)} %copy-done, f32[8,28,2,384]{3,0,2,1:T(8,128)} %copy-done.3, f32[8,28,28,2]{3,0,2,1:T(8,128)} %copy.68), kind=kLoop, calls=%fused_computation.2 | loop fusion | flops 14525952 | bytes 29102080 | tf_op jit(solution)/shard_map/concatenate | solution.py:22
  134.5 11.0 %slice.110 = f32[8,28,28,384]{3,0,2,1:T(8,128)} slice(f32[8,28,28,386]{3,0,2,1:T(8,128)} %get-tuple-element.16), slice={[0:8], [0:28], [0:28], [2:386]} | slice | bytes 19267584 | tf_op jit(solution)/shard_map/slice | solution.py:55
  145.5 8.1 slice.108
  153.6 36.5 %reshape.84 = f32[8,28,28,16,24]{4,3,0,2,1:T(8,128)} reshape(f32[8,28,28,384]{3,0,2,1:T(8,128)} %slice.108) | data formatting | bytes 19267584 | tf_op jit(solution)/shard_map/reshape | solution.py:54
  190.1 36.5 %reshape.86 = f32[8,28,28,16,24]{4,3,0,2,1:T(8,128)} reshape(f32[8,28,28,384]{3,0,2,1:T(8,128)} %slice.110) | data formatting | bytes 19267584 | tf_op jit(solution)/shard_map/reshape | solution.py:55
  226.7 34.9 %slice.111 = f32[8,28,28,16,2]{4,3,0,2,1:T(8,128)} slice(f32[8,28,28,16,24]{4,3,0,2,1:T(8,128)} %reshape.86), slice={[0:8], [0:28], [0:28], [0:16], [22:24]} | slice | bytes 1605632 | tf_op jit(solution)/shard_map/slice | solution.py:55
  261.5 77.3 %maximum_bitcast_fusion = f32[16,8,28,28,28]{4,0,1,3,2:T(8,128)} fusion(f32[8,28,28,16,2]{4,3,0,2,1:T(8,128)} %slice.111, f32[8,28,28,16,24]{4,3,0,2,1:T(8,128)} %reshape.85, f32[8,28,28,16,2]{4,3,0,2,1:T(8,128)} %bitcast.66), kind=kLoop, calls=%fused_computation | loop fusion | flops 5619712 | bytes 22478848 | tf_op jit(solution)/shard_map/transpose | solution.py:58
  338.8 6.2 fusion.29
  345.0 7.2 fusion.28
  352.2 30.2 %slice.112 = f32[16,8,24,24,24]{4,0,1,3,2:T(8,128)} slice(f32[16,8,28,28,28]{4,0,1,3,2:T(8,128)} %maximum_bitcast_fusion), slice={[0:16], [0:8], [2:26], [2:26], [2:26]} | slice | bytes 14155776 | tf_op jit(solution)/shard_map/slice | solution.py:60
  382.4 52.3 %fusion.27 = (f32[16,8,24,24,2]{4,0,1,3,2:T(8,128)}, f32[16,8,24,24,2]{4,0,1,3,2:T(8,128)}) fusion(f32[16,8,28,28,28]{4,0,1,3,2:T(8,128)} %maximum_bitcast_fusion), kind=kLoop, calls=%fused_computation.54 | loop fusion | bytes 2359296 | tf_op jit(solution)/shard_map/slice | solution.py:66
  439.0 3.7 copy.75
  442.7 2.4 reshape.88
  445.1 4.3 copy.78
  449.5 6.3 reshape.91
  455.8 4.3 copy.77
  460.1 5.9 reshape.90
  466.0 35.5 %copy.74 = f32[16,8,24,24,24]{4,3,2,1,0:T(8,128)} copy(f32[16,8,24,24,24]{4,0,1,3,2:T(8,128)} %slice.112) | data formatting | bytes 14155776 | tf_op jit(solution)/shard_map/slice | solution.py:60
  501.4 28.9 %reshape.87 = f32[16,8,13824]{2,1,0:T(8,128)} reshape(f32[16,8,24,24,24]{4,3,2,1,0:T(8,128)} %copy.74) | data formatting | bytes 14155776 | tf_op jit(solution)/shard_map/reshape | solution.py:68
  530.3 6.5 constant_dynamic-update-slice_fusion.9
  536.8 31.7 %copy.80 = f32[16,8,24,24,2]{0,1,4,3,2:T(8,128)} copy(f32[16,8,24,24,2]{4,0,1,3,2:T(8,128)} %get-tuple-element.10) | data formatting | bytes 1179648 | tf_op jit(solution)/shard_map/slice | solution.py:66
  568.5 3.3 copy.82
  571.8 31.8 %copy.79 = f32[16,8,24,24,2]{0,1,4,3,2:T(8,128)} copy(f32[16,8,24,24,2]{4,0,1,3,2:T(8,128)} %get-tuple-element.11) | data formatting | bytes 1179648 | tf_op jit(solution)/shard_map/slice | solution.py:65
  603.5 3.4 copy.81
  612.1 14.7 %fusion.2 = f32[4,4,8,20736]{3,1,2,0:T(4,128)} fusion(s32[4,4]{1,0:T(4,128)S(1)} %copy-done.15, s32[16]{0:T(128)S(1)} %copy-done.17, f32[2,8,8,20736]{3,2,1,0:T(8,128)} %bitcast.68), kind=kOutput, calls=%fused_computation.7 | convolution fusion | flops 509608192 | bytes 21233792 | tf_op jit(solution)/shard_map/bs,bv->sv/dot_general | solution.py:84
  626.8 6.1 all-to-all-start.2
  634.3 115.0 %all-to-all-done.2 = f32[4,4,8,20736]{3,1,2,0:T(4,128)} async-done(((f32[4,4,8,20736]{3,1,2,0:T(4,128)}), f32[4,4,8,20736]{3,1,2,0:T(4,128)}, u32[]{:S(2)}, u32[]{:S(2)}) %all-to-all-start.2) | async-done | bytes 10616864 | tf_op jit(solution)/shard_map/all_to_all | solution.py:93
  749.2 3.4 all-to-all-start.1
  752.6 10.2 copy.84
  762.8 6.1 all-to-all-start.3
  769.2 26.4 %sqrt_reduce_fusion = f32[24,24,384]{2,1,0:T(8,128)} fusion(f32[8,24,24,384]{3,0,2,1:T(8,128)} %copy-done.1, f32[8,28,28,386]{3,0,2,1:T(8,128)} %get-tuple-element.17, f32[8,28,28,386]{3,0,2,1:T(8,128)} %get-tuple-element.16, f32[8,28,24,384]{3,0,2,1:T(8,128)} %copy-done, f32[8,28,2,384]{3,0,2,1:T(8,128)S(1)} %copy-done.4, ...), kind=kLoop, calls=%fused_computation.29 | loop fusion | flops 116563968 | bytes 32931840 | tf_op jit(solution)/shard_map/reduce_max | solution.py:50
  795.6 203.7 %all-to-all-done.3 = f32[4,4,8,20736]{3,2,0,1:T(8,128)} async-done(((f32[4,4,8,20736]{3,2,0,1:T(8,128)}), f32[4,4,8,20736]{3,2,0,1:T(8,128)}, u32[]{:S(2)}, u32[]{:S(2)}) %all-to-all-start.3) | async-done | bytes 10616864 | tf_op jit(solution)/shard_map/all_to_all | solution.py:92
  999.3 4.7 copy.85
  1004.0 10.2 convolution_bitcast_fusion
  1014.2 14.3 %copy.87 = f32[1,1,16,8,20736]{4,3,2,1,0:T(8,128)} copy(f32[1,1,16,8,20736]{4,2,3,1,0:T(8,128)} %convolution_bitcast_fusion) | data formatting | bytes 21233664
  (71 shorter events, 22.9 us)
Async XLA Ops:
  0.6 26.3 %copy-start.2 = (f32[8,24,24,384]{3,2,1,0:T(8,128)S(1)}, f32[8,24,24,384]{3,2,1,0:T(8,128)}, u32[]{:S(2)}) copy-start(f32[8,24,24,384]{3,2,1,0:T(8,128)} %param.3) | copy-start | bytes 21233668
  7.9 4.1 copy-start.1
  8.0 18.1 %collective-permute-start.1 = (f32[8,2,24,384]{3,0,2,1:T(8,128)S(1)}, f32[8,2,24,384]{3,0,2,1:T(8,128)S(1)}, u32[]{:S(2)}, u32[]{:S(2)}) collective-permute-start(f32[8,2,24,384]{3,0,2,1:T(8,128)S(1)} %get-tuple-element.23), channel_id=1, source_target_pairs={{0,8},{8,16},{16,24},{24,0},{1,9},{9,17},{17,25},{25,1},{2,10},{10... | collective-permute-start | bytes 1769480 | tf_op jit(solution)/shard_map/ppermute | solution.py:20
  11.0 27.2 %collective-permute-start = (f32[8,2,24,384]{3,0,2,1:T(8,128)S(1)}, f32[8,2,24,384]{3,0,2,1:T(8,128)S(1)}, u32[]{:S(2)}, u32[]{:S(2)}) collective-permute-start(f32[8,2,24,384]{3,0,2,1:T(8,128)S(1)} %get-tuple-element.22), channel_id=1, source_target_pairs={{8,0},{16,8},{24,16},{0,24},{9,1},{17,9},{25,17},{1,25},{10,2},{18... | collective-permute-start | bytes 1769480 | tf_op jit(solution)/shard_map/ppermute | solution.py:21
  26.1 0.8 copy-start.11
  27.0 15.2 %copy-start.18 = (s32[1,1,16]{2,1,0:T(1,128)S(1)}, s32[1,1,16]{2,1,0:T(1,128)}, u32[]{:S(2)}) copy-start(s32[1,1,16]{2,1,0:T(1,128)} %param.4) | copy-start | bytes 196
  27.0 15.9 %copy-start.19 = (s32[1,1,16]{2,1,0:T(1,128)S(1)}, s32[1,1,16]{2,1,0:T(1,128)}, u32[]{:S(2)}) copy-start(s32[1,1,16]{2,1,0:T(1,128)} %param.5) | copy-start | bytes 196
  38.2 3.5 copy-start.13
  38.2 3.3 copy-start
  41.6 6.0 collective-permute-start.3
  41.7 5.9 collective-permute-start.2
  42.3 0.5 copy-start.16
  43.6 583.2 %all-to-all-start = ((s32[4,1,4]{2,1,0:T(1,128)}), s32[4,1,4]{2,1,0:T(1,128)}, u32[]{:S(2)}, u32[]{:S(2)}) async-start(s32[4,1,4]{2,1,0:T(1,128)} %bitcast.2), calls=%async_computation | async-start | bytes 4096 | tf_op jit(solution)/shard_map/all_to_all | solution.py:106
  47.6 0.8 copy-start.3
  48.4 0.8 copy-start.5
  68.7 43.5 %collective-permute-start.5 = (f32[8,28,28,2]{2,0,3,1:T(8,128)S(1)}, f32[8,28,28,2]{2,0,3,1:T(8,128)}, u32[]{:S(2)}, u32[]{:S(2)}) collective-permute-start(f32[8,28,28,2]{2,0,3,1:T(8,128)S(1)} %copy.67), channel_id=1, source_target_pairs={{0,1},{1,2},{2,3},{3,0},{4,5},{5,6},{6,7},{7,4},{8,9},{9,10},{10,1... | collective-permute-start | bytes 150536 | tf_op jit(solution)/shard_map/ppermute | solution.py:20
  70.3 39.4 %collective-permute-start.4 = (f32[8,28,28,2]{2,0,3,1:T(8,128)}, f32[8,28,28,2]{2,0,3,1:T(8,128)}, u32[]{:S(2)}, u32[]{:S(2)}) collective-permute-start(f32[8,28,28,2]{2,0,3,1:T(8,128)} %copy.64), channel_id=1, source_target_pairs={{1,0},{2,1},{3,2},{0,3},{5,4},{6,5},{7,6},{4,7},{9,8},{10,9},{11,1... | collective-permute-start | bytes 150536 | tf_op jit(solution)/shard_map/ppermute | solution.py:21
  571.7 35.2 %copy-start.9 = (f32[16,8,1152]{2,1,0:T(8,128)S(1)}, f32[16,8,1152]{2,1,0:T(8,128)}, u32[]{:S(2)}) copy-start(f32[16,8,1152]{2,1,0:T(8,128)} %reshape.88) | copy-start | bytes 1769476
  571.8 36.0 %copy-start.7 = (f32[16,8,1152]{2,1,0:T(8,128)S(1)}, f32[16,8,1152]{2,1,0:T(8,128)}, u32[]{:S(2)}) copy-start(f32[16,8,1152]{2,1,0:T(8,128)} %reshape.89) | copy-start | bytes 1769476
  603.5 5.1 copy-start.10
  603.5 6.0 copy-start.8
  603.5 8.5 copy-start.15
  603.5 8.5 copy-start.17
  626.8 122.4 %all-to-all-start.2 = ((f32[4,4,8,20736]{3,1,2,0:T(4,128)}), f32[4,4,8,20736]{3,1,2,0:T(4,128)}, u32[]{:S(2)}, u32[]{:S(2)}) async-start(f32[4,4,8,20736]{3,1,2,0:T(4,128)} %fusion.2), calls=%async_computation.2 | async-start | bytes 21233664 | tf_op jit(solution)/shard_map/all_to_all | solution.py:93
  749.2 13.6 %all-to-all-start.1 = ((s32[4,4,1]{0,2,1:T(1,128)}), s32[4,4,1]{0,2,1:T(1,128)S(1)}, u32[]{:S(2)}, u32[]{:S(2)}) async-start(s32[4,4,1]{0,2,1:T(1,128)} %copy.72), calls=%async_computation.1 | async-start | bytes 4096 | tf_op jit(solution)/shard_map/all_to_all | solution.py:105
  762.8 6.4 copy-start.4
  762.8 6.4 copy-start.6
  762.8 6.4 copy-start.12
  762.8 6.4 copy-start.14
  762.8 236.5 %all-to-all-start.3 = ((f32[4,4,8,20736]{3,2,0,1:T(8,128)}), f32[4,4,8,20736]{3,2,0,1:T(8,128)}, u32[]{:S(2)}, u32[]{:S(2)}) async-start(f32[4,4,8,20736]{3,2,0,1:T(8,128)} %copy.84), calls=%async_computation.3 | async-start | bytes 21233664 | tf_op jit(solution)/shard_map/all_to_all | solution.py:92
where the time goes:
time: 1040 us; the launch traced here: 1030 us
  local copies, waits for them, and re-layouts  504 us (48%)
  waiting for transfers between devices  339 us (33%)
  other arithmetic  132 us (13%)
  starting transfers between devices  28 us (3%)
  matrix products  24.9 us (2%)
    all_to_all x1, waiting for transfers between devices, per_device(): lax.all_to_all(lax.all_to_all(outgoing.reshape(width_x, slots_total // wi...  204 us
    all_to_all x1, waiting for transfers between devices, per_device(): lax.all_to_all(outgoing.reshape(width_x, slots_total // width_x, count_f,...  115 us
    slice x2, local copies, waits for them, and re-layouts, per_device(): window[:, :, 2:-2, 2:-2, -2:]  84 us
    transpose x1, other arithmetic, per_device(): jnp.concatenate([lower_z, core, upper_z], axis=4).transpose(3, 0, 1, 2, 4)  77.3 us
    slice x2, local copies, waits for them, and re-layouts, per_device(): window[:, :, 2:-2, 2:-2, 2:-2]  65.7 us
    reshape x7, local copies, waits for them, and re-layouts, per_device(): piece.reshape(block_count, count_f, -1)  52.6 us
    slice x2, local copies, waits for them, and re-layouts, per_device(): padded[:, :, :, 4:4 + depth]  45.9 us
    unnamed x50, local copies, waits for them, and re-layouts  43.2 us
  transfers between devices with their start and end apart: 10, of which 4 were waited for; matrix products, arithmetic and copies ran while one was open for 60% of the time, Pallas kernels for 0%

commit v1 on v0

v1 whole, which is shorter than its diff:
```python
import functools

import jax
import jax.numpy as jnp
from jax import lax
from jax.experimental import pallas as pl
from jax.experimental.pallas import tpu as pltpu
from jax.sharding import PartitionSpec as P

BS = 24
WIDTH = 2
AHEAD = 4
FAR_WINDOW, NEAR_WINDOW = 2, 3
TAIL = 128
GROUP = ("gx", "gz")

filter_weight = 0.01
base_term = 0.1


def block_transpose(rows, count, lanes):
    depth = count * BS
    place = lanes // BS
    skewed = [rows[0]] + [pltpu.roll(rows[r], BS * r, 1) for r in range(1, count)]
    held = [skewed[-j % count] for j in range(count)]
    step = 1
    while step < count:
        moves = (place & step) != 0
        held = [jnp.where(moves, held[(j - step) % count], held[j]) for j in range(count)]
        step *= 2
    return [held[0]] + [pltpu.roll(held[k], depth - BS * k, 1) for k in range(1, count)]


def load_rows(ref, x, start):
    return jnp.swapaxes(ref[:, x, pl.ds(start, 8), :], 0, 1)


def offset_of(owner, me, size):
    return owner ^ me if size & (size - 1) == 0 else lax.rem(owner - me + size, size)


def core_kernel(wide, fields_ref, owner_ref, slot_ref, *refs):
    count = owner_ref.shape[-1]
    outs = refs[:count]
    x_low, x_high, y_low, y_high, cells, held, labels, owners, slots = refs[count:-3]
    in_sems, fetch_sems, out_sems = refs[-3:]
    me = lax.axis_index("gx") * lax.axis_size("gz") + lax.axis_index("gz")
    size = lax.axis_size("gx") * lax.axis_size("gz")
    count_f, side_x, side_y, depth = fields_ref.shape
    steps = side_x // wide
    part = wide * side_y * BS

    def load(step):
        planes = pl.ds(step * wide, wide)
        return pltpu.make_async_copy(fields_ref.at[:, planes], cells.at[:, planes], in_sems.at[step])

    def stores(step):
        slot = lax.rem(step, 2)
        at = pl.ds(pl.multiple_of(step * part, 128), part)
        return [
            pltpu.make_async_copy(held.at[slot, d], outs[d].at[:, at], out_sems.at[slot, d])
            for d in range(count)
        ]

    fetches = [
        pltpu.make_async_copy(owner_ref, owners, fetch_sems.at[0]),
        pltpu.make_async_copy(slot_ref, slots, fetch_sems.at[1]),
    ]
    for fetch in fetches:
        fetch.start()
    for step in range(steps):
        load(step).start()
    for fetch in fetches:
        fetch.wait()
    dests = [offset_of(owners[0, 0, k], me, size) for k in range(count)]
    for k in range(count):
        labels[dests[k]] = jnp.full((count_f, TAIL), slots[0, 0, k].astype(jnp.float32))
    tails = [
        pltpu.make_async_copy(
            labels.at[d], outs[d].at[:, pl.ds(outs[d].shape[1] - TAIL, TAIL)], out_sems.at[2, d]
        )
        for d in range(count)
    ]
    for tail in tails:
        tail.start()
    lanes = lax.broadcasted_iota(jnp.int32, (count_f, depth), 1)
    tiles = [(x, start) for x in range(wide) for start in range(0, side_y, 8)]
    per_group = count // 8

    def one_step(step, carry):
        load(step).wait()

        @pl.when(step > 1)
        def _():
            for copy in stores(step - 2):
                copy.wait()

        now = lax.rem(step, 2)
        for group in range(len(tiles) // per_group):
            rows = []
            for x, start in tiles[group * per_group : (group + 1) * per_group]:
                tile = load_rows(cells, step * wide + x, start)
                for r in range(8):
                    y = start + r
                    rows.append(tile[r])
                    if y < WIDTH:
                        y_low[(step * wide + x) * WIDTH + y] = tile[r]
                    if y >= side_y - WIDTH:
                        y_high[(step * wide + x) * WIDTH + y - (side_y - WIDTH)] = tile[r]
            for k, piece in enumerate(block_transpose(rows, count, lanes)):
                held[now, dests[k], :, pl.ds(group * depth, depth)] = piece
        for copy in stores(step):
            copy.start()
        return carry

    lax.fori_loop(0, steps, one_step, 0)
    for x in range(WIDTH):
        for start in range(0, side_y, 8):
            at = pl.ds(x * side_y + start, 8)
            x_low[at] = load_rows(cells, x, start)
            x_high[at] = load_rows(cells, side_x - WIDTH + x, start)
    for step in (steps - 2, steps - 1):
        for copy in stores(step):
            copy.wait()
    for tail in tails:
        tail.wait()


def edge_kernel(fields_ref, rows_ref, low_ref, high_ref, first_ref, last_ref, low_rows, high_rows):
    count_f, wide, side_y, depth = fields_ref.shape
    count = depth // BS
    lanes = lax.broadcasted_iota(jnp.int32, (count_f, depth), 1)
    slot = lanes % BS // WIDTH
    per = BS // WIDTH

    def one_x(x, carry):
        low = high = None
        for start in range(0, side_y, 8):
            tile = load_rows(fields_ref, x, start)
            rows_ref[x, pl.ds(start, 8)] = tile
            for r in range(8):
                y = start + r
                i = y % per
                moved = tile[r] if i == 0 else pltpu.roll(tile[r], WIDTH * i, 1)
                if i == 0:
                    high = low = moved
                else:
                    high = jnp.where(slot == i, moved, high)
                    low = jnp.where(slot == i - 1, moved, low)
                if i == per - 1:
                    high_rows[x * (side_y // per) + y // per] = high
                    low_rows[x * (side_y // per) + y // per] = pltpu.roll(low, WIDTH, 1)
        return carry

    lax.fori_loop(0, wide, one_x, 0)
    lows = block_transpose([low_rows[r] for r in range(count)], count, lanes)
    for k in range(count):
        low_ref[k] = lows[k]
    last_ref[...] = lows[0]
    highs = block_transpose([high_rows[r] for r in range(count)], count, lanes)
    for k in range(count):
        high_ref[(k - 1) % count] = highs[k]
    first_ref[...] = highs[0]


def halo_kernel(
    start, dest_ref, x_low, x_high, y_low, y_high, z_low, z_high, before_z, after_z, *refs
):
    count = dest_ref.shape[0]
    outs, held, sems = refs[-count - 2 : -2], refs[-2], refs[-1]
    row_count, count_f, depth = x_low.shape
    lanes = lax.broadcasted_iota(jnp.int32, (count_f, depth), 1)
    piece_len = row_count * BS
    for n, ref in enumerate((x_low, x_high, y_low, y_high)):

        def one_group(group, carry, ref=ref, n=n):
            rows = [ref[group * count + r] for r in range(count)]
            at = pl.multiple_of(n * piece_len + group * depth, 128)
            for k, piece in enumerate(block_transpose(rows, count, lanes)):
                held[dest_ref[k], :, pl.ds(at, depth)] = piece
            return carry

        lax.fori_loop(0, row_count // count, one_group, 0)
    for k in range(count):
        low = before_z[...] if k == 0 else z_low[k]
        high = after_z[...] if k == count - 1 else z_high[k]
        held[dest_ref[k], :, pl.ds(4 * piece_len, piece_len)] = low
        held[dest_ref[k], :, pl.ds(5 * piece_len, piece_len)] = high
    copies = []
    for d in range(count):
        length = held.shape[2]
        at = pl.ds(0 if outs[d].shape[1] == length else start, length)
        copies.append(pltpu.make_async_copy(held.at[d], outs[d].at[:, at], sems.at[d]))
        copies[d].start()
    for copy in copies:
        copy.wait()


def axis_terms(lower, center, upper):
    ahead = (upper - center) * 0.5
    behind = (center - lower) * 0.5
    second = (ahead - behind) * 0.5
    spread = (
        jnp.abs(ahead)
        + jnp.abs(behind)
        + filter_weight * (jnp.abs(upper) + 2.0 * jnp.abs(center) + jnp.abs(lower))
        + base_term
    )
    return (second * second, spread * spread)


def indicator_kernel(
    prev_ref, rows_ref, next_ref, y_low, y_high, before_z, after_z, *refs
):
    out_ref, held = refs[-2:]
    wide, side_y, count_f, depth = rows_ref.shape
    lanes = lax.broadcasted_iota(jnp.int32, (count_f, depth), 1)
    held[0:WIDTH] = prev_ref[...]
    held[WIDTH : WIDTH + wide] = rows_ref[...]
    held[WIDTH + wide :] = next_ref[...]

    def one_x(x, carry):
        shift = lax.rem(depth - x * (side_y * WIDTH), depth)
        before = pltpu.roll(before_z[...], shift, 1)
        after = pltpu.roll(after_z[...], shift, 1)
        for y in range(side_y):
            center = held[x + WIDTH, y]
            num, den = axis_terms(held[x, y], center, held[x + 2 * WIDTH, y])
            behind = y_low[x, y] if y < WIDTH else held[x + WIDTH, y - WIDTH]
            past = y + WIDTH - side_y
            ahead = y_high[x, past] if past >= 0 else held[x + WIDTH, y + WIDTH]
            num_y, den_y = axis_terms(behind, center, ahead)
            behind = jnp.where(
                lanes < WIDTH,
                pltpu.roll(before, depth - WIDTH * y, 1) if y else before,
                pltpu.roll(center, WIDTH, 1),
            )
            ahead = jnp.where(
                lanes >= depth - WIDTH,
                pltpu.roll(after, depth - WIDTH - WIDTH * y, 1),
                pltpu.roll(center, depth - WIDTH, 1),
            )
            num_z, den_z = axis_terms(behind, center, ahead)
            ratio = (num + num_y + num_z) / (den + den_y + den_z)
            out_ref[x, pl.ds(y, 1), :] = jnp.sqrt(jnp.max(ratio, axis=0, keepdims=True))
        return carry

    lax.fori_loop(0, wide, one_x, 0)


def place_kernel(count, has_base, *refs):
    arrays = refs[:count]
    out, slots = refs[count + has_base : count + has_base + 2]
    held, sems = refs[-count - 1 : -1], refs[-1]
    fetches = [pltpu.make_async_copy(arrays[n], held[n], sems.at[0, n]) for n in range(count)]
    for fetch in fetches:
        fetch.start()
    copies = []
    for n in range(count):
        length = arrays[n].shape[1] - TAIL
        fetches[n].wait()
        slot = jnp.max(held[n][:, pl.ds(length, TAIL)]).astype(jnp.int32)
        slots[n] = slot
        at = pl.ds(0, length)
        copies.append(
            pltpu.make_async_copy(held[n].at[:, at], out.at[slot, :, at], sems.at[1, n])
        )
        copies[n].start()
    for copy in copies:
        copy.wait()


def place(arrays, shape, base=None):
    count = len(arrays)
    has_base = 0 if base is None else 1
    hbm = pl.BlockSpec(memory_space=pltpu.HBM)
    return pl.pallas_call(
        functools.partial(place_kernel, count, has_base),
        out_shape=[
            jax.ShapeDtypeStruct(shape, jnp.float32),
            jax.ShapeDtypeStruct((count,), jnp.int32),
        ],
        in_specs=[pl.BlockSpec(memory_space=pl.ANY)] * count + [hbm] * has_base,
        out_specs=[hbm, pl.BlockSpec(memory_space=pltpu.SMEM)],
        scratch_shapes=[pltpu.VMEM(array.shape, jnp.float32) for array in arrays]
        + [pltpu.SemaphoreType.DMA((2, count))],
        input_output_aliases={count: 0} if has_base else {},
        compiler_params=pltpu.CompilerParams(vmem_limit_bytes=60 * 2**20),
    )(*arrays, *([base] if has_base else []))


def place_halos_kernel(start, count, slots_ref, *refs):
    arrays = refs[:count]
    out, sems = refs[count + 1 :]
    length = arrays[0].shape[1]
    copies = [
        pltpu.make_async_copy(arrays[n], out.at[slots_ref[n], :, pl.ds(start, length)], sems.at[n])
        for n in range(count)
    ]
    for copy in copies:
        copy.start()
    for copy in copies:
        copy.wait()


def place_halos(start, slots, arrays, placed):
    count = len(arrays)
    hbm = pl.BlockSpec(memory_space=pltpu.HBM)
    return pl.pallas_call(
        functools.partial(place_halos_kernel, start, count),
        out_shape=jax.ShapeDtypeStruct(placed.shape, jnp.float32),
        in_specs=[pl.BlockSpec(memory_space=pltpu.SMEM)]
        + [pl.BlockSpec(memory_space=pltpu.VMEM)] * count
        + [hbm],
        out_specs=hbm,
        scratch_shapes=[pltpu.SemaphoreType.DMA((count,))],
        input_output_aliases={1 + count: 0},
        compiler_params=pltpu.CompilerParams(vmem_limit_bytes=12 * 2**20),
    )(slots, *arrays, placed)


def send_order(width_x, width_z):
    xs = [0, 3, 1, 2] if width_x == 4 else list(range(width_x))
    half = width_z // 2
    far = [x * width_z + z for x in xs for z in reversed(range(half, width_z))]
    near = [x * width_z + z for x in reversed(range(width_x)) for z in reversed(range(half))]
    return far, [d for d in near if d]


def ring(axis, move):
    size = lax.axis_size(axis)
    return [(i, (i + move) % size) for i in range(size)]


def per_device(fields, new_owner, new_slot):
    count_f, side_x, side_y, depth = fields.shape
    count = depth // BS
    width_x, width_z = lax.axis_size("gx"), lax.axis_size("gz")
    size = width_x * width_z
    is_power = size & (size - 1) == 0
    me = lax.axis_index(GROUP).astype(jnp.int32)
    dest = offset_of(new_owner.reshape(count), me, size)

    far, near = send_order(width_x, width_z)
    split = far[:AHEAD]
    core_len = side_x * side_y * BS
    halo_len = 12 * BS * side_y
    wide = 4
    part = wide * side_y * BS
    halo_rows = WIDTH * side_y
    row_shape = jax.ShapeDtypeStruct((halo_rows, count_f, depth), jnp.float32)
    hbm = pl.BlockSpec(memory_space=pltpu.HBM)
    whole = pl.BlockSpec(memory_space=pltpu.VMEM)
    *core, x_first, x_last, y_first, y_last = pl.pallas_call(
        functools.partial(core_kernel, wide),
        out_shape=[
            jax.ShapeDtypeStruct(
                (count_f, core_len + (0 if d in split else halo_len) + TAIL), jnp.float32
            )
            for d in range(count)
        ]
        + [row_shape] * 4,
        in_specs=[hbm, hbm, hbm],
        out_specs=[hbm] * count + [whole] * 4,
        scratch_shapes=[
            pltpu.VMEM(fields.shape, jnp.float32),
            pltpu.VMEM((2, count, count_f, part), jnp.float32),
            pltpu.VMEM((count, count_f, TAIL), jnp.float32),
            pltpu.SMEM(new_owner.shape, jnp.int32),
            pltpu.SMEM(new_owner.shape, jnp.int32),
            pltpu.SemaphoreType.DMA((side_x // wide,)),
            pltpu.SemaphoreType.DMA((2,)),
            pltpu.SemaphoreType.DMA((3, count)),
        ],
        compiler_params=pltpu.CompilerParams(vmem_limit_bytes=60 * 2**20),
        cost_estimate=pl.CostEstimate(flops=0, bytes_accessed=32 * 2**20, transcendentals=0),
    )(fields, new_owner, new_slot)

    span = 8
    z_shape = jax.ShapeDtypeStruct((count, count_f, halo_rows * BS), jnp.float32)
    edge_shape = jax.ShapeDtypeStruct((count_f, halo_rows * BS), jnp.float32)
    z_block = pl.BlockSpec((count, count_f, depth), lambda i: (0, 0, i))
    edge_block = pl.BlockSpec((count_f, depth), lambda i: (0, i))
    rows_block = pl.BlockSpec((span, side_y, count_f, depth), lambda i: (i, 0, 0, 0))
    rows, z_low, z_high, z_first, z_last = pl.pallas_call(
        edge_kernel,
        out_shape=[
            jax.ShapeDtypeStruct((side_x, side_y, count_f, depth), jnp.float32),
            z_shape,
            z_shape,
            edge_shape,
            edge_shape,
        ],
        grid=(side_x // span,),
        in_specs=[pl.BlockSpec((count_f, span, side_y, depth), lambda i: (0, i, 0, 0))],
        out_specs=[rows_block, z_block, z_block, edge_block, edge_block],
        scratch_shapes=[pltpu.VMEM((count, count_f, depth), jnp.float32)] * 2,
        compiler_params=pltpu.CompilerParams(vmem_limit_bytes=60 * 2**20),
        cost_estimate=pl.CostEstimate(flops=0, bytes_accessed=32 * 2**20, transcendentals=0),
    )(fields)

    values = {("core", d): core[d] for d in split}
    values |= {"x_up": x_last, "x_down": x_first, "y_up": y_last, "y_down": y_first}
    values |= {"z_up": z_last, "z_down": z_first}
    arrived = {}

    def start(name, *after):
        value = values[name]
        if after:
            value, *_ = lax.optimization_barrier((value, *after))
        if isinstance(name, str):
            axis = "g" + name[0]
            pairs = ring(axis, 1 if name.endswith("up") else -1)
        else:
            axis, d = GROUP, name[1]
            move = (lambda s: s ^ d) if is_power else (lambda s: (s + d) % size)
            pairs = [(s, move(s)) for s in range(size)]
        arrived[name] = lax.ppermute(value, axis, pairs)

    far_chain, near_chain = [], []

    def start_far(name, *after):
        past = [arrived[far_chain[-FAR_WINDOW]]] if len(far_chain) >= FAR_WINDOW else []
        start(name, *past, *after)
        far_chain.append(name)

    def start_near(name, *after):
        past = [arrived[near_chain[-NEAR_WINDOW]]] if len(near_chain) >= NEAR_WINDOW else []
        start(name, *past, *after)
        near_chain.append(name)

    for d in split:
        start_far(("core", d))
    for name in ("x_up", "y_up", "x_down", "y_down", "z_up", "z_down"):
        start_near(name)
    x_low, x_high = arrived["x_up"], arrived["x_down"]
    y_low, y_high = arrived["y_up"], arrived["y_down"]
    before_z, after_z = arrived["z_up"], arrived["z_down"]

    full = [d for d in range(size) if d not in split]
    halos = pl.pallas_call(
        functools.partial(halo_kernel, core_len),
        out_shape=[
            jax.ShapeDtypeStruct((count_f, halo_len) if d in split else core[d].shape, jnp.float32)
            for d in range(count)
        ],
        in_specs=[pl.BlockSpec(memory_space=pltpu.SMEM)] + [whole] * 8 + [hbm] * len(full),
        out_specs=[hbm] * count,
        input_output_aliases={9 + n: d for n, d in enumerate(full)},
        scratch_shapes=[
            pltpu.VMEM((count, count_f, halo_len), jnp.float32),
            pltpu.SemaphoreType.DMA((count,)),
        ],
        compiler_params=pltpu.CompilerParams(vmem_limit_bytes=60 * 2**20),
        cost_estimate=pl.CostEstimate(flops=0, bytes_accessed=32 * 2**20, transcendentals=0),
    )(
        dest, x_low, x_high, y_low, y_high, z_low, z_high, before_z, after_z,
        *[core[d] for d in full],
    )
    parts = side_x // span
    per_span = span // WIDTH
    side_block = (WIDTH, side_y, count_f, depth)
    indicators = []
    for n in range(parts):

        def at(block, *index):
            return pl.BlockSpec(block, lambda i: index)

        prev, prev_at = (rows, n * per_span - 1) if n else (x_low.reshape(side_block), 0)
        last = n == parts - 1
        next, next_at = (x_high.reshape(side_block), 0) if last else (rows, (n + 1) * per_span)
        y_block = at((span, WIDTH, count_f, depth), n, 0, 0, 0)
        z_part = at((count_f, depth), 0, n)
        indicators.append(
            pl.pallas_call(
                indicator_kernel,
                out_shape=jax.ShapeDtypeStruct((side_x, side_y, depth), jnp.float32),
                grid=(1,),
                in_specs=[
                    at(side_block, prev_at, 0, 0, 0),
                    at((span, side_y, count_f, depth), n, 0, 0, 0),
                    at(side_block, next_at, 0, 0, 0),
                    y_block,
                    y_block,
                    z_part,
                    z_part,
                ]
                + [hbm] * (n > 0),
                out_specs=at((span, side_y, depth), n, 0, 0),
                scratch_shapes=[
                    pltpu.VMEM((span + 2 * WIDTH, side_y, count_f, depth), jnp.float32)
                ],
                input_output_aliases={7: 0} if n else {},
                compiler_params=pltpu.CompilerParams(vmem_limit_bytes=60 * 2**20),
                cost_estimate=pl.CostEstimate(
                    flops=10**8, bytes_accessed=16 * 2**20, transcendentals=0
                ),
            )(
                prev,
                rows,
                next,
                y_low.reshape(side_x, WIDTH, count_f, depth),
                y_high.reshape(side_x, WIDTH, count_f, depth),
                before_z,
                after_z,
                *indicators[-1:],
            )
        )

    values |= {("halo" if d in split else "all", d): halos[d] for d in range(size)}
    far_rest = [("all", d) for d in far[AHEAD:]] + [("halo", d) for d in split]
    beside = dict(zip(far_rest[len(far_rest) - parts - len(split) + 1 :], indicators))
    shape = (count, count_f, core_len + halo_len)
    placed, slots = place([arrived["core", d] for d in split], shape)
    beside[far_rest[-len(split) // 2]] = slots
    for name in far_rest:
        start_far(name, *([beside[name]] if name in beside else []))
    for d in near:
        start_near(("all", d))
    placed, _ = place([halos[0]] + [arrived["all", d] for d in full if d], shape, placed)
    placed = place_halos(core_len, slots, [arrived["halo", d] for d in split], placed)
    return (indicators[-1], placed.reshape((1, 1) + shape))


def solution(mesh):
    placed = (P(None, "gx", "gy", "gz"), P("gx", "gy", "gz"), P("gx", "gy", "gz"))
    return jax.shard_map(
        per_device,
        mesh=mesh,
        in_specs=placed,
        out_specs=(P("gx", "gy", "gz"), P("gx", "gy", "gz", None, None)),
        check_vma=False,
    )
```

time: 1040 us -> 276 us (0.27)
  local copies, waits for them, and re-layouts: 504 us -> 1.73 us
  waiting for transfers between devices: 339 us -> 140 us
  other arithmetic: 132 us -> 0.57 us
  Pallas kernels: 0 us -> 68.5 us
  starting transfers between devices: 28 us -> 62.5 us
  matrix products: 24.9 us -> 0 us
    all_to_all x4 -> x0, waiting for transfers between devices: 319 us -> none  [the longest x1 204 us: per_device(): lax.all_to_all(lax.all_to_all(outgoing.reshape(width_x, slots_total // wi...]
    slice x19 -> x0, local copies, waits for them, and re-layouts: 274 us -> none  [the longest x2 84 us: per_device(): window[:, :, 2:-2, 2:-2, -2:]]
    reshape x10 -> x0, local copies, waits for them, and re-layouts: 162 us -> none  [the longest x7 52.6 us: per_device(): piece.reshape(block_count, count_f, -1)]
    ppermute x6 -> x25, waiting for transfers between devices: 20.7 us -> 140 us  [start(): arrived[name] = lax.ppermute(value, axis, pairs)]
    transpose x1 -> x0, other arithmetic: 77.3 us -> none  [per_device(): jnp.concatenate([lower_z, core, upper_z], axis=4).transpose(3, 0, 1, 2, 4)]
    pallas_call x0 -> x9, Pallas kernels: none -> 68.5 us  [the longest x3 29.2 us: per_device(): pl.pallas_call(indicator_kernel, out_shape=jax.ShapeDtypeStruct((side_x,...]
    ppermute x6 -> x25, starting transfers between devices: 8.45 us -> 62.5 us  [start(): arrived[name] = lax.ppermute(value, axis, pairs)]
    unnamed x50 -> x36, local copies, waits for them, and re-layouts: 43.2 us -> 1.73 us
  transfers between devices with their start and end apart: 10 -> 25, of which waited for: 4 -> 11; matrix products, arithmetic and copies ran while one was open for 60% -> 0% of each run, Pallas kernels for 0% -> 20%
where the time goes in v1:
time: 276 us; the launch traced here: 274 us
  waiting for transfers between devices  140 us (51%)
  Pallas kernels  68.5 us (25%)
  starting transfers between devices  62.5 us (23%)
    ppermute x25, waiting for transfers between devices, start(): arrived[name] = lax.ppermute(value, axis, pairs)  140 us
    ppermute x25, starting transfers between devices, start(): arrived[name] = lax.ppermute(value, axis, pairs)  62.5 us
    pallas_call x3, Pallas kernels, per_device(): pl.pallas_call(indicator_kernel, out_shape=jax.ShapeDtypeStruct((side_x,...  29.2 us
    pallas_call x1, Pallas kernels, per_device(): pl.pallas_call(functools.partial(core_kernel, wide), out_shape=[jax.Shape...  11 us
    pallas_call x1, Pallas kernels, per_device(): pl.pallas_call(edge_kernel, out_shape=[jax.ShapeDtypeStruct((side_x, side...  10.3 us
    pallas_call x2, Pallas kernels, place(): pl.pallas_call(functools.partial(place_kernel, count, has_base), out_shap...  9.8 us
    pallas_call x1, Pallas kernels, per_device(): pl.pallas_call(functools.partial(halo_kernel, core_len), out_shape=[jax.S...  6.74 us
  transfers between devices with their start and end apart: 25, of which 11 were waited for; matrix products, arithmetic and copies ran while one was open for 0% of the time, Pallas kernels for 20%

profile of v1, /device:TPU:0, one launch (start us, length us, event | category | flops | bytes accessed | tf_op | source)
XLA Modules:
  0.0 274.4 jit_solution(3746950802559273880)
XLA Ops:
  0.6 11.0 %shard_map.51 = (f32[8,20864]{1,0:T(8,128)}, f32[8,20864]{1,0:T(8,128)}, f32[8,13952]{1,0:T(8,128)}, f32[8,13952]{1,0:T(8,128)}, f32[8,20864]{1,0:T(8,128)}, /*i...) custom-call(f32[8,24,24,384]{3,2,1,0:T(8,128)} %fields_ref.3, ...), custom_call_target="tpu_custom_call" | custom-call | bytes 33554432 | tf_op jit(solution)/shard_map/pallas_call | solution.py:354
  11.6 3.0 %collective-permute-start.2 = (f32[48,8,384]{2,1,0:T(8,128)}, f32[48,8,384]{2,1,0:T(8,128)S(1)}, u32[]{:S(2)}, u32[]{:S(2)}) collective-permute-start(f32[48,8,384]{2,1,0:T(8,128)} %get-tuple-element.70), channel_id=1, source_target_pairs={{0,8},{8,16},{16,24},{24,0},{1,9},{9,17},{17,25},{25,1},{2,10},{10... | collective-permute-start | bytes 1769480 | tf_op jit(solution)/shard_map/ppermute | solution.py:418
  14.6 1.0 collective-permute-start
  15.6 0.0 collective-permute-start.1
  15.6 4.0 %collective-permute-start.6 = (f32[8,13952]{1,0:T(8,128)}, f32[8,13952]{1,0:T(8,128)S(1)}, u32[]{:S(2)}, u32[]{:S(2)}) collective-permute-start(f32[8,13952]{1,0:T(8,128)} %get-tuple-element.76), channel_id=1, source_target_pairs={{0,3},{1,2},{2,1},{3,0},{8,11},{9,10},{10,9},{11,8},{16,19},{17,18... | collective-permute-start | bytes 1339400 | tf_op jit(solution)/shard_map/ppermute | solution.py:418
  19.7 0.0 collective-permute-start.7
  19.7 10.3 %collective-permute-done.2.x_low = f32[48,8,384]{2,1,0:T(8,128)S(1)} collective-permute-done((f32[48,8,384]{2,1,0:T(8,128)}, f32[48,8,384]{2,1,0:T(8,128)S(1)}, u32[]{:S(2)}, u32[]{:S(2)}) %collective-permute-start.2) | collective-permute-done | bytes 589856 | tf_op jit(solution)/shard_map/ppermute | solution.py:418
  29.9 1.1 collective-permute-done.6.refs_0_
  31.1 4.7 %collective-permute-start.8 = (f32[8,13952]{1,0:T(8,128)}, f32[8,13952]{1,0:T(8,128)}, u32[]{:S(2)}, u32[]{:S(2)}) collective-permute-start(f32[8,13952]{1,0:T(8,128)} %get-tuple-element.79), channel_id=1, source_target_pairs={{0,27},{1,26},{2,25},{3,24},{8,19},{9,18},{10,17},{11,16},{16,11},... | collective-permute-start | bytes 1339400 | tf_op jit(solution)/shard_map/ppermute | solution.py:418
  35.8 10.3 %shard_map.50 = (f32[24,24,8,384]{3,2,1,0:T(8,128)}, f32[16,8,1152]{2,1,0:T(8,128)}, f32[16,8,1152]{2,1,0:T(8,128)}, f32[8,1152]{1,0:T(8,128)}, f32[8,1152]{1,0:T(8,128)}) custom-call(f32[8,24,24,384]{3,2,1,0:T(8,128)} %fields_ref.3), custom_call_target="tpu_custom_call" | custom-call | bytes 33554432 | tf_op jit(solution)/shard_map/pallas_call | solution.py:385
  46.1 22.5 %collective-permute-done.7.refs_1_ = f32[8,13952]{1,0:T(8,128)S(1)} collective-permute-done((f32[8,13952]{1,0:T(8,128)}, f32[8,13952]{1,0:T(8,128)S(1)}, u32[]{:S(2)}, u32[]{:S(2)}) %collective-permute-start.7) | collective-permute-done | bytes 446496 | tf_op jit(solution)/shard_map/ppermute | solution.py:418
  68.6 4.6 %collective-permute-start.9 = (f32[8,13952]{1,0:T(8,128)}, f32[8,13952]{1,0:T(8,128)}, u32[]{:S(2)}, u32[]{:S(2)}) collective-permute-start(f32[8,13952]{1,0:T(8,128)} %get-tuple-element.81), channel_id=1, source_target_pairs={{0,26},{1,27},{2,24},{3,25},{8,18},{9,19},{10,16},{11,17},{16,10},... | collective-permute-start | bytes 1339400 | tf_op jit(solution)/shard_map/ppermute | solution.py:418
  73.2 0.0 collective-permute-done.x_high
  73.2 2.5 collective-permute-start.5
  75.7 0.6 xor_bitcast_fusion.dest_ref
  76.3 7.2 %collective-permute-done.5.after_z = f32[8,1152]{1,0:T(8,128)S(1)} collective-permute-done((f32[8,1152]{1,0:T(8,128)}, f32[8,1152]{1,0:T(8,128)S(1)}, u32[]{:S(2)}, u32[]{:S(2)}) %collective-permute-start.5) | collective-permute-done | bytes 36896 | tf_op jit(solution)/shard_map/ppermute | solution.py:418
  83.5 3.2 %collective-permute-done.4.before_z = f32[8,1152]{1,0:T(8,128)S(1)} collective-permute-done((f32[8,1152]{1,0:T(8,128)}, f32[8,1152]{1,0:T(8,128)S(1)}, u32[]{:S(2)}, u32[]{:S(2)}) %collective-permute-start.4) | collective-permute-done | bytes 36896 | tf_op jit(solution)/shard_map/ppermute | solution.py:418
  86.7 0.0 collective-permute-done.3.y_high
  86.8 0.6 copy-done.12
  87.4 0.2 copy-done.2
  87.6 6.7 %shard_map.56 = (f32[8,20864]{1,0:T(8,128)}, f32[8,20864]{1,0:T(8,128)}, f32[8,6912]{1,0:T(8,128)}, f32[8,6912]{1,0:T(8,128)}, f32[8,20864]{1,0:T(8,128)}, /*ind...) custom-call(s32[16]{0:T(128)} %xor_bitcast_fusion.dest_ref, ...), custom_call_target="tpu_custom_call", output_to_operand_aliasing={{0}: (9, {}), {1}: (10, {}), {4}: (11, {}), {5}: (12, {}), ... | custom-call | bytes 33554432 | tf_op jit(solution)/shard_map/pallas_call | solution.py:441
  94.3 13.4 %collective-permute-start.18 = (f32[8,20864]{1,0:T(8,128)}, f32[8,20864]{1,0:T(8,128)}, u32[]{:S(2)}, u32[]{:S(2)}) collective-permute-start(f32[8,20864]{1,0:T(8,128)} %get-tuple-element.117), channel_id=1, source_target_pairs={{0,25},{1,24},{2,27},{3,26},{8,17},{9,16},{10,19},{11,18},{16,9},{... | collective-permute-start | bytes 2002952 | tf_op jit(solution)/shard_map/ppermute | solution.py:418
  107.7 0.0 collective-permute-done.8.refs_2_
  107.7 3.3 %collective-permute-start.10 = (f32[8,20864]{1,0:T(8,128)}, f32[8,20864]{1,0:T(8,128)S(1)}, u32[]{:S(2)}, u32[]{:S(2)}) collective-permute-start(f32[8,20864]{1,0:T(8,128)} %get-tuple-element.100), channel_id=1, source_target_pairs={{0,11},{1,10},{2,9},{3,8},{8,3},{9,2},{10,1},{11,0},{16,27},{17,26... | collective-permute-start | bytes 2002952 | tf_op jit(solution)/shard_map/ppermute | solution.py:418
  111.1 0.5 collective-permute-start.23
  111.6 3.8 %collective-permute-start.21 = (f32[8,20864]{1,0:T(8,128)}, f32[8,20864]{1,0:T(8,128)}, u32[]{:S(2)}, u32[]{:S(2)}) collective-permute-start(f32[8,20864]{1,0:T(8,128)} %get-tuple-element.122), channel_id=1, source_target_pairs={{0,17},{1,16},{2,19},{3,18},{8,25},{9,24},{10,27},{11,26},{16,1},{... | collective-permute-start | bytes 2002952 | tf_op jit(solution)/shard_map/ppermute | solution.py:418
  115.4 20.2 %collective-permute-done.18.refs_11_ = f32[8,20864]{1,0:T(8,128)} collective-permute-done((f32[8,20864]{1,0:T(8,128)}, f32[8,20864]{1,0:T(8,128)}, u32[]{:S(2)}, u32[]{:S(2)}) %collective-permute-start.18) | collective-permute-done | bytes 667680 | tf_op jit(solution)/shard_map/ppermute | solution.py:418
  135.6 0.4 collective-permute-start.19
  136.0 9.7 %shard_map.52.refs_0_ = f32[24,24,384]{2,1,0:T(8,128)} custom-call(f32[2,24,8,384]{3,2,1,0:T(8,128)} %bitcast.15, f32[24,24,8,384]{3,2,1,0:T(8,128)} %get-tuple-element.66.rows_ref.next_ref.prev_ref, f32[24,24,8,384]{3,2,1,0:T(8,128)} %get-tuple-element.66.rows_ref.next_ref.prev_ref, f32[24,2,8,384]{3,2,1,0:T(8,128)} %bitcast.8, f32[24,2,8,384]{3,2,1,0:T(8,128)} %bitcast.11, ...), custom_call_target="tpu_custom_call" | custom-call | flops 100000000 | bytes 16777216 | tf_op jit(solution)/shard_map/pallas_call | solution.py:475
  145.6 7.9 %collective-permute-done.10.refs_5_ = f32[8,20864]{1,0:T(8,128)S(1)} collective-permute-done((f32[8,20864]{1,0:T(8,128)}, f32[8,20864]{1,0:T(8,128)S(1)}, u32[]{:S(2)}, u32[]{:S(2)}) %collective-permute-start.10) | collective-permute-done | bytes 667680 | tf_op jit(solution)/shard_map/ppermute | solution.py:418
  153.6 0.9 copy-done.10
  154.5 9.8 %shard_map.53.refs_0_ = f32[24,24,384]{2,1,0:T(8,128)} custom-call(f32[24,24,8,384]{3,2,1,0:T(8,128)} %get-tuple-element.66.rows_ref.next_ref.prev_ref, f32[24,24,8,384]{3,2,1,0:T(8,128)} %get-tuple-element.66.rows_ref.next_ref.prev_ref, f32[24,24,8,384]{3,2,1,0:T(8,128)} %get-tuple-element.66.rows_ref.next_ref.prev_ref, ...), custom_call_target="tpu_custom_call", output_to_operand_aliasing={{}: (7, {})} | custom-call | flops 100000000 | bytes 16777216 | tf_op jit(solution)/shard_map/pallas_call | solution.py:475
  164.3 14.0 %collective-permute-done.13.refs_4_ = f32[8,20864]{1,0:T(8,128)} collective-permute-done((f32[8,20864]{1,0:T(8,128)}, f32[8,20864]{1,0:T(8,128)}, u32[]{:S(2)}, u32[]{:S(2)}) %collective-permute-start.13) | collective-permute-done | bytes 667680 | tf_op jit(solution)/shard_map/ppermute | solution.py:418
  178.3 0.8 collective-permute-start.14
  179.1 3.4 %collective-permute-start.11 = (f32[8,20864]{1,0:T(8,128)S(1)}, f32[8,20864]{1,0:T(8,128)}, u32[]{:S(2)}, u32[]{:S(2)}) collective-permute-start(f32[8,20864]{1,0:T(8,128)S(1)} %copy-done.9), channel_id=1, source_target_pairs={{0,19},{1,18},{2,17},{3,16},{8,27},{9,26},{10,25},{11,24},{16,3},{... | collective-permute-start | bytes 2002952 | tf_op jit(solution)/shard_map/ppermute | solution.py:418
  182.6 0.6 collective-permute-start.24
  183.2 1.4 collective-permute-start.22
  184.6 8.8 %collective-permute-start.20 = (f32[8,20864]{1,0:T(8,128)S(1)}, f32[8,20864]{1,0:T(8,128)}, u32[]{:S(2)}, u32[]{:S(2)}) collective-permute-start(f32[8,20864]{1,0:T(8,128)S(1)} %copy-done.5), channel_id=1, source_target_pairs={{0,1},{1,0},{2,3},{3,2},{8,9},{9,8},{10,11},{11,10},{16,17},{17,16... | collective-permute-start | bytes 2002952 | tf_op jit(solution)/shard_map/ppermute | solution.py:418
  193.4 9.7 %shard_map.54 = f32[24,24,384]{2,1,0:T(8,128)} custom-call(f32[24,24,8,384]{3,2,1,0:T(8,128)} %get-tuple-element.66.rows_ref.next_ref.prev_ref, f32[24,24,8,384]{3,2,1,0:T(8,128)} %get-tuple-element.66.rows_ref.next_ref.prev_ref, f32[2,24,8,384]{3,2,1,0:T(8,128)} %bitcast.14, f32[24,2,8,384]{3,2,1,0:T(8,128)} %bitcast.10, ...), custom_call_target="tpu_custom_call", output_to_operand_aliasing={{}: (7, {})} | custom-call | flops 100000000 | bytes 16777216 | tf_op jit(solution)/shard_map/pallas_call | solution.py:475
  203.1 22.4 %collective-permute-done.14.refs_8_ = f32[8,20864]{1,0:T(8,128)} collective-permute-done((f32[8,20864]{1,0:T(8,128)S(1)}, f32[8,20864]{1,0:T(8,128)}, u32[]{:S(2)}, u32[]{:S(2)}) %collective-permute-start.14) | collective-permute-done | bytes 667680 | tf_op jit(solution)/shard_map/ppermute | solution.py:418
  225.5 1.6 collective-permute-start.12
  227.1 2.9 %shard_map.55 = (f32[16,8,20736]{2,1,0:T(8,128)}, s32[4]{0:T(128)}) custom-call(f32[8,13952]{1,0:T(8,128)} %copy-done.13, f32[8,13952]{1,0:T(8,128)} %copy-done.14, f32[8,13952]{1,0:T(8,128)} %collective-permute-done.8.refs_2_, f32[8,13952]{1,0:T(8,128)} %collective-permute-done.9.refs_3_), custom_call_target="tpu_custom_call" | custom-call | tf_op jit(solution)/shard_map/pallas_call | solution.py:277
  230.0 22.4 %collective-permute-done.15.refs_1_ = f32[8,6912]{1,0:T(8,128)S(1)} collective-permute-done((f32[8,6912]{1,0:T(8,128)}, f32[8,6912]{1,0:T(8,128)S(1)}, u32[]{:S(2)}, u32[]{:S(2)}) %collective-permute-start.15) | collective-permute-done | bytes 221216 | tf_op jit(solution)/shard_map/ppermute | solution.py:418
  252.4 1.2 collective-permute-start.17
  253.6 3.4 %collective-permute-start.16 = (f32[8,6912]{1,0:T(8,128)S(1)}, f32[8,6912]{1,0:T(8,128)S(1)}, u32[]{:S(2)}, u32[]{:S(2)}) collective-permute-start(f32[8,6912]{1,0:T(8,128)S(1)} %copy-done.16), channel_id=1, source_target_pairs={{0,27},{1,26},{2,25},{3,24},{8,19},{9,18},{10,17},{11,16},{16,11},... | collective-permute-start | bytes 663560 | tf_op jit(solution)/shard_map/ppermute | solution.py:418
  257.1 6.9 %shard_map.57 = (f32[16,8,20736]{2,1,0:T(8,128)}, s32[12]{0:T(128)}) custom-call(f32[8,20864]{1,0:T(8,128)} %get-tuple-element.113.refs_0_, f32[8,20864]{1,0:T(8,128)} %collective-permute-done.20.refs_1_, f32[8,20864]{1,0:T(8,128)} %collective-permute-done.22.refs_2_, f32[8,20864]{1,0:T(8,128)} %collective-permute-done.24.refs_3_, ...), custom_call_target="tpu_custom_call", output_to_operand_aliasing={{0}: (12, {})} | custom-call | tf_op jit(solution)/shard_map/pallas_call | solution.py:277
  264.0 9.0 %collective-permute-done.17.refs_3_ = f32[8,6912]{1,0:T(8,128)S(1)} collective-permute-done((f32[8,6912]{1,0:T(8,128)S(1)}, f32[8,6912]{1,0:T(8,128)S(1)}, u32[]{:S(2)}, u32[]{:S(2)}) %collective-permute-start.17) | collective-permute-done | bytes 221216 | tf_op jit(solution)/shard_map/ppermute | solution.py:418
  272.9 1.5 shard_map.58
  (48 shorter events, 0.1 us)
Async XLA Ops:
  0.6 75.1 %copy-start.15 = (s32[1,1,16]{2,1,0:T(1,128)S(1)}, s32[1,1,16]{2,1,0:T(1,128)}, u32[]{:S(2)}) copy-start(s32[1,1,16]{2,1,0:T(1,128)} %owner_ref.1) | copy-start | bytes 196
  11.6 18.3 %collective-permute-start.2 = (f32[48,8,384]{2,1,0:T(8,128)}, f32[48,8,384]{2,1,0:T(8,128)S(1)}, u32[]{:S(2)}, u32[]{:S(2)}) collective-permute-start(f32[48,8,384]{2,1,0:T(8,128)} %get-tuple-element.70), channel_id=1, source_target_pairs={{0,8},{8,16},{16,24},{24,0},{1,9},{9,17},{17,25},{25,1},{2,10},{10... | collective-permute-start | bytes 1769480 | tf_op jit(solution)/shard_map/ppermute | solution.py:418
  14.6 58.6 %collective-permute-start = (f32[48,8,384]{2,1,0:T(8,128)}, f32[48,8,384]{2,1,0:T(8,128)S(1)}, u32[]{:S(2)}, u32[]{:S(2)}) collective-permute-start(f32[48,8,384]{2,1,0:T(8,128)} %get-tuple-element.67), channel_id=1, source_target_pairs={{0,24},{8,0},{16,8},{24,16},{1,25},{9,1},{17,9},{25,17},{2,26},{10... | collective-permute-start | bytes 1769480 | tf_op jit(solution)/shard_map/ppermute | solution.py:418
  15.6 60.1 %collective-permute-start.1 = (f32[48,8,384]{2,1,0:T(8,128)}, f32[48,8,384]{2,1,0:T(8,128)S(1)}, u32[]{:S(2)}, u32[]{:S(2)}) collective-permute-start(f32[48,8,384]{2,1,0:T(8,128)} %get-tuple-element.68), channel_id=1, source_target_pairs={{0,4},{4,0},{1,5},{5,1},{2,6},{6,2},{3,7},{7,3},{8,12},{12,8},{9,1... | collective-permute-start | bytes 1769480 | tf_op jit(solution)/shard_map/ppermute | solution.py:418
  15.6 15.4 %collective-permute-start.6 = (f32[8,13952]{1,0:T(8,128)}, f32[8,13952]{1,0:T(8,128)S(1)}, u32[]{:S(2)}, u32[]{:S(2)}) collective-permute-start(f32[8,13952]{1,0:T(8,128)} %get-tuple-element.76), channel_id=1, source_target_pairs={{0,3},{1,2},{2,1},{3,0},{8,11},{9,10},{10,9},{11,8},{16,19},{17,18... | collective-permute-start | bytes 1339400 | tf_op jit(solution)/shard_map/ppermute | solution.py:418
  19.7 48.9 %collective-permute-start.7 = (f32[8,13952]{1,0:T(8,128)}, f32[8,13952]{1,0:T(8,128)S(1)}, u32[]{:S(2)}, u32[]{:S(2)}) collective-permute-start(f32[8,13952]{1,0:T(8,128)} %get-tuple-element.77), channel_id=1, source_target_pairs={{0,2},{1,3},{2,0},{3,1},{8,10},{9,11},{10,8},{11,9},{16,18},{17,19... | collective-permute-start | bytes 1339400 | tf_op jit(solution)/shard_map/ppermute | solution.py:418
  29.9 56.8 %copy-start.4 = (f32[48,8,384]{2,1,0:T(8,128)}, f32[48,8,384]{2,1,0:T(8,128)S(1)}, u32[]{:S(2)}) copy-start(f32[48,8,384]{2,1,0:T(8,128)S(1)} %collective-permute-done.2.x_low) | copy-start | bytes 1769476
  29.9 56.8 %collective-permute-start.3 = (f32[48,8,384]{2,1,0:T(8,128)}, f32[48,8,384]{2,1,0:T(8,128)S(1)}, u32[]{:S(2)}, u32[]{:S(2)}) collective-permute-start(f32[48,8,384]{2,1,0:T(8,128)} %get-tuple-element.71), channel_id=1, source_target_pairs={{0,4},{4,0},{1,5},{5,1},{2,6},{6,2},{3,7},{7,3},{8,12},{12,8},{9,1... | collective-permute-start | bytes 1769480 | tf_op jit(solution)/shard_map/ppermute | solution.py:418
  31.1 114.6 %copy-start.13 = (f32[8,13952]{1,0:T(8,128)}, f32[8,13952]{1,0:T(8,128)S(1)}, u32[]{:S(2)}) copy-start(f32[8,13952]{1,0:T(8,128)S(1)} %collective-permute-done.6.refs_0_) | copy-start | bytes 1339396
  31.1 76.7 %collective-permute-start.8 = (f32[8,13952]{1,0:T(8,128)}, f32[8,13952]{1,0:T(8,128)}, u32[]{:S(2)}, u32[]{:S(2)}) collective-permute-start(f32[8,13952]{1,0:T(8,128)} %get-tuple-element.79), channel_id=1, source_target_pairs={{0,27},{1,26},{2,25},{3,24},{8,19},{9,18},{10,17},{11,16},{16,11},... | collective-permute-start | bytes 1339400 | tf_op jit(solution)/shard_map/ppermute | solution.py:418
  68.6 85.0 %copy-start.14 = (f32[8,13952]{1,0:T(8,128)}, f32[8,13952]{1,0:T(8,128)S(1)}, u32[]{:S(2)}) copy-start(f32[8,13952]{1,0:T(8,128)S(1)} %collective-permute-done.7.refs_1_) | copy-start | bytes 1339396
  68.6 42.5 %collective-permute-start.9 = (f32[8,13952]{1,0:T(8,128)}, f32[8,13952]{1,0:T(8,128)}, u32[]{:S(2)}, u32[]{:S(2)}) collective-permute-start(f32[8,13952]{1,0:T(8,128)} %get-tuple-element.81), channel_id=1, source_target_pairs={{0,26},{1,27},{2,24},{3,25},{8,18},{9,19},{10,16},{11,17},{16,10},... | collective-permute-start | bytes 1339400 | tf_op jit(solution)/shard_map/ppermute | solution.py:418
  73.2 13.5 %copy-start.3 = (f32[48,8,384]{2,1,0:T(8,128)}, f32[48,8,384]{2,1,0:T(8,128)S(1)}, u32[]{:S(2)}) copy-start(f32[48,8,384]{2,1,0:T(8,128)S(1)} %collective-permute-done.x_high) | copy-start | bytes 1769476
  73.2 10.3 %collective-permute-start.5 = (f32[8,1152]{1,0:T(8,128)}, f32[8,1152]{1,0:T(8,128)S(1)}, u32[]{:S(2)}, u32[]{:S(2)}) collective-permute-start(f32[8,1152]{1,0:T(8,128)} %get-tuple-element.75), channel_id=1, source_target_pairs={{0,3},{1,0},{2,1},{3,2},{4,7},{5,4},{6,5},{7,6},{8,11},{9,8},{10,9... | collective-permute-start | bytes 110600 | tf_op jit(solution)/shard_map/ppermute | solution.py:418
  75.7 11.0 %copy-start.1 = (f32[48,8,384]{2,1,0:T(8,128)}, f32[48,8,384]{2,1,0:T(8,128)S(1)}, u32[]{:S(2)}) copy-start(f32[48,8,384]{2,1,0:T(8,128)S(1)} %collective-permute-done.1.y_low) | copy-start | bytes 1769476
  75.7 11.0 %collective-permute-start.4 = (f32[8,1152]{1,0:T(8,128)}, f32[8,1152]{1,0:T(8,128)S(1)}, u32[]{:S(2)}, u32[]{:S(2)}) collective-permute-start(f32[8,1152]{1,0:T(8,128)} %get-tuple-element.73), channel_id=1, source_target_pairs={{0,1},{1,2},{2,3},{3,0},{4,5},{5,6},{6,7},{7,4},{8,9},{9,10},{10,1... | collective-permute-start | bytes 110600 | tf_op jit(solution)/shard_map/ppermute | solution.py:418
  83.5 3.3 %copy-start.11 = (f32[8,1152]{1,0:T(8,128)}, f32[8,1152]{1,0:T(8,128)S(1)}, u32[]{:S(2)}) copy-start(f32[8,1152]{1,0:T(8,128)S(1)} %collective-permute-done.5.after_z) | copy-start | bytes 110596
  86.7 0.6 copy-start.12
  86.7 0.8 copy-start.2
  94.3 41.2 %collective-permute-start.18 = (f32[8,20864]{1,0:T(8,128)}, f32[8,20864]{1,0:T(8,128)}, u32[]{:S(2)}, u32[]{:S(2)}) collective-permute-start(f32[8,20864]{1,0:T(8,128)} %get-tuple-element.117), channel_id=1, source_target_pairs={{0,25},{1,24},{2,27},{3,26},{8,17},{9,16},{10,19},{11,18},{16,9},{... | collective-permute-start | bytes 2002952 | tf_op jit(solution)/shard_map/ppermute | solution.py:418
  107.7 45.8 %collective-permute-start.10 = (f32[8,20864]{1,0:T(8,128)}, f32[8,20864]{1,0:T(8,128)S(1)}, u32[]{:S(2)}, u32[]{:S(2)}) collective-permute-start(f32[8,20864]{1,0:T(8,128)} %get-tuple-element.100), channel_id=1, source_target_pairs={{0,11},{1,10},{2,9},{3,8},{8,3},{9,2},{10,1},{11,0},{16,27},{17,26... | collective-permute-start | bytes 2002952 | tf_op jit(solution)/shard_map/ppermute | solution.py:418
  111.1 67.3 %collective-permute-start.13 = (f32[8,20864]{1,0:T(8,128)}, f32[8,20864]{1,0:T(8,128)}, u32[]{:S(2)}, u32[]{:S(2)}) collective-permute-start(f32[8,20864]{1,0:T(8,128)} %get-tuple-element.106), channel_id=1, source_target_pairs={{0,10},{1,11},{2,8},{3,9},{8,2},{9,3},{10,0},{11,1},{16,26},{17,27... | collective-permute-start | bytes 2002952 | tf_op jit(solution)/shard_map/ppermute | solution.py:418
  111.1 71.5 %collective-permute-start.23 = (f32[8,20864]{1,0:T(8,128)}, f32[8,20864]{1,0:T(8,128)}, u32[]{:S(2)}, u32[]{:S(2)}) collective-permute-start(f32[8,20864]{1,0:T(8,128)} %get-tuple-element.126), channel_id=1, source_target_pairs={{0,24},{1,25},{2,26},{3,27},{8,16},{9,17},{10,18},{11,19},{16,8},{... | collective-permute-start | bytes 2002952 | tf_op jit(solution)/shard_map/ppermute | solution.py:418
  111.6 71.5 %collective-permute-start.21 = (f32[8,20864]{1,0:T(8,128)}, f32[8,20864]{1,0:T(8,128)}, u32[]{:S(2)}, u32[]{:S(2)}) collective-permute-start(f32[8,20864]{1,0:T(8,128)} %get-tuple-element.122), channel_id=1, source_target_pairs={{0,17},{1,16},{2,19},{3,18},{8,25},{9,24},{10,27},{11,26},{16,1},{... | collective-permute-start | bytes 2002952 | tf_op jit(solution)/shard_map/ppermute | solution.py:418
  135.6 49.0 %collective-permute-start.19 = (f32[8,20864]{1,0:T(8,128)}, f32[8,20864]{1,0:T(8,128)}, u32[]{:S(2)}, u32[]{:S(2)}) collective-permute-start(f32[8,20864]{1,0:T(8,128)} %get-tuple-element.118), channel_id=1, source_target_pairs={{0,16},{1,17},{2,18},{3,19},{8,24},{9,25},{10,26},{11,27},{16,0},{... | collective-permute-start | bytes 2002952 | tf_op jit(solution)/shard_map/ppermute | solution.py:418
  153.6 0.9 copy-start.10
  154.4 23.9 %copy-start.8 = (f32[8,20864]{1,0:T(8,128)S(1)}, f32[8,20864]{1,0:T(8,128)}, u32[]{:S(2)}) copy-start(f32[8,20864]{1,0:T(8,128)} %get-tuple-element.107) | copy-start | bytes 2002948
  154.4 24.7 %copy-start.9 = (f32[8,20864]{1,0:T(8,128)S(1)}, f32[8,20864]{1,0:T(8,128)}, u32[]{:S(2)}) copy-start(f32[8,20864]{1,0:T(8,128)} %get-tuple-element.101) | copy-start | bytes 2002948
  154.4 28.1 %copy-start.7 = (f32[8,20864]{1,0:T(8,128)S(1)}, f32[8,20864]{1,0:T(8,128)}, u32[]{:S(2)}) copy-start(f32[8,20864]{1,0:T(8,128)} %get-tuple-element.127) | copy-start | bytes 2002948
  154.4 28.7 %copy-start.6 = (f32[8,20864]{1,0:T(8,128)S(1)}, f32[8,20864]{1,0:T(8,128)}, u32[]{:S(2)}) copy-start(f32[8,20864]{1,0:T(8,128)} %get-tuple-element.123) | copy-start | bytes 2002948
  154.4 30.2 %copy-start.5 = (f32[8,20864]{1,0:T(8,128)S(1)}, f32[8,20864]{1,0:T(8,128)}, u32[]{:S(2)}) copy-start(f32[8,20864]{1,0:T(8,128)} %get-tuple-element.119) | copy-start | bytes 2002948
  164.3 88.1 %copy-start.17 = (f32[8,6912]{1,0:T(8,128)S(1)}, f32[8,6912]{1,0:T(8,128)}, u32[]{:S(2)}) copy-start(f32[8,6912]{1,0:T(8,128)} %get-tuple-element.112) | copy-start | bytes 663556
  164.3 89.3 %copy-start.16 = (f32[8,6912]{1,0:T(8,128)S(1)}, f32[8,6912]{1,0:T(8,128)}, u32[]{:S(2)}) copy-start(f32[8,6912]{1,0:T(8,128)} %get-tuple-element.110) | copy-start | bytes 663556
  178.3 47.2 %collective-permute-start.14 = (f32[8,20864]{1,0:T(8,128)S(1)}, f32[8,20864]{1,0:T(8,128)}, u32[]{:S(2)}, u32[]{:S(2)}) collective-permute-start(f32[8,20864]{1,0:T(8,128)S(1)} %copy-done.8), channel_id=1, source_target_pairs={{0,18},{1,19},{2,16},{3,17},{8,26},{9,27},{10,24},{11,25},{16,2},{... | collective-permute-start | bytes 2002952 | tf_op jit(solution)/shard_map/ppermute | solution.py:418
  179.1 46.4 %collective-permute-start.11 = (f32[8,20864]{1,0:T(8,128)S(1)}, f32[8,20864]{1,0:T(8,128)}, u32[]{:S(2)}, u32[]{:S(2)}) collective-permute-start(f32[8,20864]{1,0:T(8,128)S(1)} %copy-done.9), channel_id=1, source_target_pairs={{0,19},{1,18},{2,17},{3,16},{8,27},{9,26},{10,25},{11,24},{16,3},{... | collective-permute-start | bytes 2002952 | tf_op jit(solution)/shard_map/ppermute | solution.py:418
  182.6 74.5 %collective-permute-start.24 = (f32[8,20864]{1,0:T(8,128)S(1)}, f32[8,20864]{1,0:T(8,128)}, u32[]{:S(2)}, u32[]{:S(2)}) collective-permute-start(f32[8,20864]{1,0:T(8,128)S(1)} %copy-done.7), channel_id=1, source_target_pairs={{0,9},{1,8},{2,11},{3,10},{8,1},{9,0},{10,3},{11,2},{16,25},{17,24... | collective-permute-start | bytes 2002952 | tf_op jit(solution)/shard_map/ppermute | solution.py:418
  183.2 73.9 %collective-permute-start.22 = (f32[8,20864]{1,0:T(8,128)S(1)}, f32[8,20864]{1,0:T(8,128)}, u32[]{:S(2)}, u32[]{:S(2)}) collective-permute-start(f32[8,20864]{1,0:T(8,128)S(1)} %copy-done.6), channel_id=1, source_target_pairs={{0,8},{1,9},{2,10},{3,11},{8,0},{9,1},{10,2},{11,3},{16,24},{17,25... | collective-permute-start | bytes 2002952 | tf_op jit(solution)/shard_map/ppermute | solution.py:418
  184.6 72.5 %collective-permute-start.20 = (f32[8,20864]{1,0:T(8,128)S(1)}, f32[8,20864]{1,0:T(8,128)}, u32[]{:S(2)}, u32[]{:S(2)}) collective-permute-start(f32[8,20864]{1,0:T(8,128)S(1)} %copy-done.5), channel_id=1, source_target_pairs={{0,1},{1,0},{2,3},{3,2},{8,9},{9,8},{10,11},{11,10},{16,17},{17,16... | collective-permute-start | bytes 2002952 | tf_op jit(solution)/shard_map/ppermute | solution.py:418
  225.5 26.9 %collective-permute-start.15 = (f32[8,6912]{1,0:T(8,128)}, f32[8,6912]{1,0:T(8,128)S(1)}, u32[]{:S(2)}, u32[]{:S(2)}) collective-permute-start(f32[8,6912]{1,0:T(8,128)} %get-tuple-element.108), channel_id=1, source_target_pairs={{0,2},{1,3},{2,0},{3,1},{8,10},{9,11},{10,8},{11,9},{16,18},{17,19... | collective-permute-start | bytes 663560 | tf_op jit(solution)/shard_map/ppermute | solution.py:418
  225.5 28.1 %collective-permute-start.12 = (f32[8,6912]{1,0:T(8,128)}, f32[8,6912]{1,0:T(8,128)S(1)}, u32[]{:S(2)}, u32[]{:S(2)}) collective-permute-start(f32[8,6912]{1,0:T(8,128)} %get-tuple-element.102), channel_id=1, source_target_pairs={{0,3},{1,2},{2,1},{3,0},{8,11},{9,10},{10,9},{11,8},{16,19},{17,18... | collective-permute-start | bytes 663560 | tf_op jit(solution)/shard_map/ppermute | solution.py:418
  230.0 42.9 %copy-start = (s32[4]{0:T(128)S(1)}, s32[4]{0:T(128)}, u32[]{:S(2)}) copy-start(s32[4]{0:T(128)} %get-tuple-element.82.slots_ref) | copy-start | bytes 52
  252.4 20.5 %collective-permute-start.17 = (f32[8,6912]{1,0:T(8,128)S(1)}, f32[8,6912]{1,0:T(8,128)S(1)}, u32[]{:S(2)}, u32[]{:S(2)}) collective-permute-start(f32[8,6912]{1,0:T(8,128)S(1)} %copy-done.17), channel_id=1, source_target_pairs={{0,26},{1,27},{2,24},{3,25},{8,18},{9,19},{10,16},{11,17},{16,10},... | collective-permute-start | bytes 663560 | tf_op jit(solution)/shard_map/ppermute | solution.py:418
  253.6 19.3 %collective-permute-start.16 = (f32[8,6912]{1,0:T(8,128)S(1)}, f32[8,6912]{1,0:T(8,128)S(1)}, u32[]{:S(2)}, u32[]{:S(2)}) collective-permute-start(f32[8,6912]{1,0:T(8,128)S(1)} %copy-done.16), channel_id=1, source_target_pairs={{0,27},{1,26},{2,25},{3,24},{8,19},{9,18},{10,17},{11,16},{16,11},... | collective-permute-start | bytes 663560 | tf_op jit(solution)/shard_map/ppermute | solution.py:418

commit v2 on v1

--- a/solution.py
+++ b/solution.py
@@ -9,7 +9,7 @@
 
 BS = 24
 WIDTH = 2
-AHEAD = 4
+AHEAD = 3
 FAR_WINDOW, NEAR_WINDOW = 2, 3
 TAIL = 128
 GROUP = ("gx", "gz")
@@ -42,7 +42,7 @@
 def core_kernel(wide, fields_ref, owner_ref, slot_ref, *refs):
     count = owner_ref.shape[-1]
     outs = refs[:count]
-    x_low, x_high, y_low, y_high, cells, held, labels, owners, slots = refs[count:-3]
+    x_low, x_high, y_ends, cells, held, labels, owners, slots = refs[count:-3]
     in_sems, fetch_sems, out_sems = refs[-3:]
     me = lax.axis_index("gx") * lax.axis_size("gz") + lax.axis_index("gz")
     size = lax.axis_size("gx") * lax.axis_size("gz")
@@ -104,9 +104,9 @@
                     y = start + r
                     rows.append(tile[r])
                     if y < WIDTH:
-                        y_low[(step * wide + x) * WIDTH + y] = tile[r]
+                        y_ends[1, (step * wide + x) * WIDTH + y] = tile[r]
                     if y >= side_y - WIDTH:
-                        y_high[(step * wide + x) * WIDTH + y - (side_y - WIDTH)] = tile[r]
+                        y_ends[0, (step * wide + x) * WIDTH + y - (side_y - WIDTH)] = tile[r]
             for k, piece in enumerate(block_transpose(rows, count, lanes)):
                 held[now, dests[k], :, pl.ds(group * depth, depth)] = piece
         for copy in stores(step):
@@ -164,14 +164,15 @@
 
 
 def halo_kernel(
-    start, dest_ref, x_low, x_high, y_low, y_high, z_low, z_high, before_z, after_z, *refs
+    start, sequence, dest_ref, x_low, x_high, y_halos, z_low, z_high, before_z, after_z, *refs
 ):
     count = dest_ref.shape[0]
-    outs, held, sems = refs[-count - 2 : -2], refs[-2], refs[-1]
+    outs = {d: refs[n - count - 2] for n, d in enumerate(sequence)}
+    held, sems = refs[-2:]
     row_count, count_f, depth = x_low.shape
     lanes = lax.broadcasted_iota(jnp.int32, (count_f, depth), 1)
     piece_len = row_count * BS
-    for n, ref in enumerate((x_low, x_high, y_low, y_high)):
+    for n, ref in enumerate((x_low, x_high, y_halos.at[0], y_halos.at[1])):
 
         def one_group(group, carry, ref=ref, n=n):
             rows = [ref[group * count + r] for r in range(count)]
@@ -327,6 +328,14 @@
     return far, [d for d in near if d]
 
 
+def interleave(first, second):
+    both = []
+    while first or second:
+        both += first[:1] + second[:1]
+        first, second = first[1:], second[1:]
+    return both
+
+
 def ring(axis, move):
     size = lax.axis_size(axis)
     return [(i, (i + move) % size) for i in range(size)]
@@ -351,7 +360,7 @@
     row_shape = jax.ShapeDtypeStruct((halo_rows, count_f, depth), jnp.float32)
     hbm = pl.BlockSpec(memory_space=pltpu.HBM)
     whole = pl.BlockSpec(memory_space=pltpu.VMEM)
-    *core, x_first, x_last, y_first, y_last = pl.pallas_call(
+    *core, x_first, x_last, y_ends = pl.pallas_call(
         functools.partial(core_kernel, wide),
         out_shape=[
             jax.ShapeDtypeStruct(
@@ -359,9 +368,10 @@
             )
             for d in range(count)
         ]
-        + [row_shape] * 4,
+        + [row_shape] * 2
+        + [jax.ShapeDtypeStruct((2,) + row_shape.shape, jnp.float32)],
         in_specs=[hbm, hbm, hbm],
-        out_specs=[hbm] * count + [whole] * 4,
+        out_specs=[hbm] * count + [whole] * 3,
         scratch_shapes=[
             pltpu.VMEM(fields.shape, jnp.float32),
             pltpu.VMEM((2, count, count_f, part), jnp.float32),
@@ -400,7 +410,7 @@
     )(fields)
 
     values = {("core", d): core[d] for d in split}
-    values |= {"x_up": x_last, "x_down": x_first, "y_up": y_last, "y_down": y_first}
+    values |= {"x_up": x_last, "x_down": x_first}
     values |= {"z_up": z_last, "z_down": z_first}
     arrived = {}
 
@@ -431,22 +441,33 @@
 
     for d in split:
         start_far(("core", d))
-    for name in ("x_up", "y_up", "x_down", "y_down", "z_up", "z_down"):
-        start_near(name)
+    start_near("x_up")
+    if lax.axis_size("gy") == 2:
+        values["y_up"] = y_ends
+        start_near("y_up")
+        y_halos = arrived["y_up"]
+    else:
+        values |= {"y_up": y_ends[0], "y_down": y_ends[1]}
+        start_near("y_up")
+        start_near("y_down")
+        y_halos = jnp.stack([arrived["y_up"], arrived["y_down"]])
+    start_near("x_down")
+    start_near("z_up")
+    start_near("z_down")
     x_low, x_high = arrived["x_up"], arrived["x_down"]
-    y_low, y_high = arrived["y_up"], arrived["y_down"]
     before_z, after_z = arrived["z_up"], arrived["z_down"]
 
-    full = [d for d in range(size) if d not in split]
+    sequence = interleave(far[AHEAD:] + split, near) + [0]
+    full = [d for d in sequence if d not in split]
     halos = pl.pallas_call(
-        functools.partial(halo_kernel, core_len),
+        functools.partial(halo_kernel, core_len, sequence),
         out_shape=[
             jax.ShapeDtypeStruct((count_f, halo_len) if d in split else core[d].shape, jnp.float32)
-            for d in range(count)
+            for d in sequence
         ],
-        in_specs=[pl.BlockSpec(memory_space=pltpu.SMEM)] + [whole] * 8 + [hbm] * len(full),
+        in_specs=[pl.BlockSpec(memory_space=pltpu.SMEM)] + [whole] * 7 + [hbm] * len(full),
         out_specs=[hbm] * count,
-        input_output_aliases={9 + n: d for n, d in enumerate(full)},
+        input_output_aliases={8 + n: sequence.index(d) for n, d in enumerate(full)},
         scratch_shapes=[
             pltpu.VMEM((count, count_f, halo_len), jnp.float32),
             pltpu.SemaphoreType.DMA((count,)),
@@ -454,7 +475,7 @@
         compiler_params=pltpu.CompilerParams(vmem_limit_bytes=60 * 2**20),
         cost_estimate=pl.CostEstimate(flops=0, bytes_accessed=32 * 2**20, transcendentals=0),
     )(
-        dest, x_low, x_high, y_low, y_high, z_low, z_high, before_z, after_z,
+        dest, x_low, x_high, y_halos, z_low, z_high, before_z, after_z,
         *[core[d] for d in full],
     )
     parts = side_x // span
@@ -469,7 +490,7 @@
         prev, prev_at = (rows, n * per_span - 1) if n else (x_low.reshape(side_block), 0)
         last = n == parts - 1
         next, next_at = (x_high.reshape(side_block), 0) if last else (rows, (n + 1) * per_span)
-        y_block = at((span, WIDTH, count_f, depth), n, 0, 0, 0)
+        y_block = (None, span, WIDTH, count_f, depth)
         z_part = at((count_f, depth), 0, n)
         indicators.append(
             pl.pallas_call(
@@ -480,8 +501,8 @@
                     at(side_block, prev_at, 0, 0, 0),
                     at((span, side_y, count_f, depth), n, 0, 0, 0),
                     at(side_block, next_at, 0, 0, 0),
-                    y_block,
-                    y_block,
+                    at(y_block, 0, n, 0, 0, 0),
+                    at(y_block, 1, n, 0, 0, 0),
                     z_part,
                     z_part,
                 ]
@@ -499,15 +520,16 @@
                 prev,
                 rows,
                 next,
-                y_low.reshape(side_x, WIDTH, count_f, depth),
-                y_high.reshape(side_x, WIDTH, count_f, depth),
+                y_halos.reshape(2, side_x, WIDTH, count_f, depth),
+                y_halos.reshape(2, side_x, WIDTH, count_f, depth),
                 before_z,
                 after_z,
                 *indicators[-1:],
             )
         )
 
-    values |= {("halo" if d in split else "all", d): halos[d] for d in range(size)}
+    halos = {d: halos[n] for n, d in enumerate(sequence)}
+    values |= {("halo" if d in split else "all", d): halos[d] for d in sequence}
     far_rest = [("all", d) for d in far[AHEAD:]] + [("halo", d) for d in split]
     beside = dict(zip(far_rest[len(far_rest) - parts - len(split) + 1 :], indicators))
     shape = (count, count_f, core_len + halo_len)

time: 276 us -> 254 us (0.920)
  waiting for transfers between devices: 140 us -> 102 us
  starting transfers between devices: 62.5 us -> 80.3 us
    ppermute x25 -> x23, waiting for transfers between devices: 140 us -> 102 us  [start(): arrived[name] = lax.ppermute(value, axis, pairs)]
    ppermute x25 -> x23, starting transfers between devices: 62.5 us -> 80.3 us  [start(): arrived[name] = lax.ppermute(value, axis, pairs)]
  transfers between devices with their start and end apart: 25 -> 23, of which waited for: 11 -> 7; matrix products, arithmetic and copies ran while one was open for 0% -> 0% of each run, Pallas kernels for 20% -> 22%
where the time goes in v2:
time: 254 us
  waiting for transfers between devices  102 us (40%)
  starting transfers between devices  80.3 us (32%)
  Pallas kernels  68.6 us (27%)
    ppermute x23, waiting for transfers between devices, start(): arrived[name] = lax.ppermute(value, axis, pairs)  102 us
    ppermute x23, starting transfers between devices, start(): arrived[name] = lax.ppermute(value, axis, pairs)  80.3 us
    pallas_call x3, Pallas kernels, per_device(): pl.pallas_call(indicator_kernel, out_shape=jax.ShapeDtypeStruct((side_x,...  29.1 us
    pallas_call x1, Pallas kernels, per_device(): pl.pallas_call(functools.partial(core_kernel, wide), out_shape=[jax.Shape...  11 us
    pallas_call x2, Pallas kernels, place(): pl.pallas_call(functools.partial(place_kernel, count, has_base), out_shap...  10.2 us
    pallas_call x1, Pallas kernels, per_device(): pl.pallas_call(edge_kernel, out_shape=[jax.ShapeDtypeStruct((side_x, side...  10.2 us
    pallas_call x1, Pallas kernels, per_device(): pl.pallas_call(functools.partial(halo_kernel, core_len, sequence), out_sh...  6.78 us
  transfers between devices with their start and end apart: 23, of which 7 were waited for; matrix products, arithmetic and copies ran while one was open for 0% of the time, Pallas kernels for 22%

profile of v2, /device:TPU:0, one launch (start us, length us, event | category | flops | bytes accessed | tf_op | source)
XLA Modules:
  0.0 253.7 jit_solution(8169218711092062464)
XLA Ops:
  0.6 11.0 %shard_map.51 = (f32[8,20864]{1,0:T(8,128)}, f32[8,20864]{1,0:T(8,128)}, f32[8,13952]{1,0:T(8,128)}, f32[8,13952]{1,0:T(8,128)}, f32[8,20864]{1,0:T(8,128)}, /*i...) custom-call(f32[8,24,24,384]{3,2,1,0:T(8,128)} %fields_ref.3, ...), custom_call_target="tpu_custom_call" | custom-call | bytes 33554432 | tf_op jit(solution)/shard_map/pallas_call | solution.py:363
  11.7 0.5 collective-permute-start.1
  12.2 2.6 %collective-permute-start.2 = (f32[48,8,384]{2,1,0:T(8,128)}, f32[48,8,384]{2,1,0:T(8,128)S(1)}, u32[]{:S(2)}, u32[]{:S(2)}) collective-permute-start(f32[48,8,384]{2,1,0:T(8,128)} %get-tuple-element.67), channel_id=1, source_target_pairs={{0,8},{8,16},{16,24},{24,0},{1,9},{9,17},{17,25},{25,1},{2,10},{10... | collective-permute-start | bytes 1769480 | tf_op jit(solution)/shard_map/ppermute | solution.py:428
  14.7 1.0 collective-permute-start
  15.8 4.0 %collective-permute-start.5 = (f32[8,13952]{1,0:T(8,128)}, f32[8,13952]{1,0:T(8,128)S(1)}, u32[]{:S(2)}, u32[]{:S(2)}) collective-permute-start(f32[8,13952]{1,0:T(8,128)} %get-tuple-element.71), channel_id=1, source_target_pairs={{0,3},{1,2},{2,1},{3,0},{8,11},{9,10},{10,9},{11,8},{16,19},{17,18... | collective-permute-start | bytes 1339400 | tf_op jit(solution)/shard_map/ppermute | solution.py:428
  19.8 0.0 collective-permute-start.6
  19.8 10.2 %shard_map.50 = (f32[24,24,8,384]{3,2,1,0:T(8,128)}, f32[16,8,1152]{2,1,0:T(8,128)}, f32[16,8,1152]{2,1,0:T(8,128)}, f32[8,1152]{1,0:T(8,128)}, f32[8,1152]{1,0:T(8,128)}) custom-call(f32[8,24,24,384]{3,2,1,0:T(8,128)} %fields_ref.3), custom_call_target="tpu_custom_call" | custom-call | bytes 33554432 | tf_op jit(solution)/shard_map/pallas_call | solution.py:395
  30.0 0.1 collective-permute-done.2.x_low
  30.1 2.0 collective-permute-start.3
  32.1 0.0 collective-permute-done.1.y_halos
  32.1 2.1 collective-permute-start.4
  34.2 0.6 xor_bitcast_fusion.dest_ref
  34.7 0.0 collective-permute-done.5.refs_0_
  34.7 2.9 %collective-permute-start.7 = (f32[8,13952]{1,0:T(8,128)}, f32[8,13952]{1,0:T(8,128)}, u32[]{:S(2)}, u32[]{:S(2)}) collective-permute-start(f32[8,13952]{1,0:T(8,128)} %get-tuple-element.74), channel_id=1, source_target_pairs={{0,27},{1,26},{2,25},{3,24},{8,19},{9,18},{10,17},{11,16},{16,11},... | collective-permute-start | bytes 1339400 | tf_op jit(solution)/shard_map/ppermute | solution.py:428
  37.7 14.6 %collective-permute-done.x_high = f32[48,8,384]{2,1,0:T(8,128)S(1)} collective-permute-done((f32[48,8,384]{2,1,0:T(8,128)}, f32[48,8,384]{2,1,0:T(8,128)S(1)}, u32[]{:S(2)}, u32[]{:S(2)}) %collective-permute-start) | collective-permute-done | bytes 589856 | tf_op jit(solution)/shard_map/ppermute | solution.py:428
  52.3 0.0 collective-permute-done.3.before_z
  52.3 0.0 collective-permute-done.4.after_z
  52.3 0.8 copy-done.2
  53.1 0.0 copy-done.13
  53.1 0.0 copy-done.14
  53.2 6.8 %shard_map.56 = (f32[8,20864]{1,0:T(8,128)}, f32[8,20864]{1,0:T(8,128)}, f32[8,20864]{1,0:T(8,128)}, f32[8,20864]{1,0:T(8,128)}, f32[8,20864]{1,0:T(8,128)}, /*i...) custom-call(s32[16]{0:T(128)} %xor_bitcast_fusion.dest_ref, ...), custom_call_target="tpu_custom_call", output_to_operand_aliasing={{0}: (8, {}), {1}: (9, {}), {2}: (10, {}), {3}: (11, {}), {... | custom-call | bytes 33554432 | tf_op jit(solution)/shard_map/pallas_call | solution.py:462
  59.9 9.5 %collective-permute-done.6.refs_1_ = f32[8,13952]{1,0:T(8,128)S(1)} collective-permute-done((f32[8,13952]{1,0:T(8,128)}, f32[8,13952]{1,0:T(8,128)S(1)}, u32[]{:S(2)}, u32[]{:S(2)}) %collective-permute-start.6) | collective-permute-done | bytes 446496 | tf_op jit(solution)/shard_map/ppermute | solution.py:428
  69.5 11.0 %collective-permute-start.11 = (f32[8,20864]{1,0:T(8,128)}, f32[8,20864]{1,0:T(8,128)S(1)}, u32[]{:S(2)}, u32[]{:S(2)}) collective-permute-start(f32[8,20864]{1,0:T(8,128)} %get-tuple-element.101), channel_id=1, source_target_pairs={{0,26},{1,27},{2,24},{3,25},{8,18},{9,19},{10,16},{11,17},{16,10},... | collective-permute-start | bytes 2002952 | tf_op jit(solution)/shard_map/ppermute | solution.py:428
  80.4 0.0 collective-permute-done.7.refs_2_
  80.5 3.0 %collective-permute-start.8 = (f32[8,20864]{1,0:T(8,128)}, f32[8,20864]{1,0:T(8,128)S(1)}, u32[]{:S(2)}, u32[]{:S(2)}) collective-permute-start(f32[8,20864]{1,0:T(8,128)} %get-tuple-element.94), channel_id=1, source_target_pairs={{0,11},{1,10},{2,9},{3,8},{8,3},{9,2},{10,1},{11,0},{16,27},{17,26... | collective-permute-start | bytes 2002952 | tf_op jit(solution)/shard_map/ppermute | solution.py:428
  83.5 28.8 %collective-permute-done.11.refs_1_ = f32[8,20864]{1,0:T(8,128)S(1)} collective-permute-done((f32[8,20864]{1,0:T(8,128)}, f32[8,20864]{1,0:T(8,128)S(1)}, u32[]{:S(2)}, u32[]{:S(2)}) %collective-permute-start.11) | collective-permute-done | bytes 667680 | tf_op jit(solution)/shard_map/ppermute | solution.py:428
  112.3 0.0 collective-permute-start.12
  112.3 22.5 %collective-permute-start.18 = (f32[8,20864]{1,0:T(8,128)}, f32[8,20864]{1,0:T(8,128)S(1)}, u32[]{:S(2)}, u32[]{:S(2)}) collective-permute-start(f32[8,20864]{1,0:T(8,128)} %get-tuple-element.113), channel_id=1, source_target_pairs={{0,17},{1,16},{2,19},{3,18},{8,25},{9,24},{10,27},{11,26},{16,1},{... | collective-permute-start | bytes 2002952 | tf_op jit(solution)/shard_map/ppermute | solution.py:428
  134.8 6.2 %collective-permute-start.19 = (f32[8,20864]{1,0:T(8,128)}, f32[8,20864]{1,0:T(8,128)}, u32[]{:S(2)}, u32[]{:S(2)}) collective-permute-start(f32[8,20864]{1,0:T(8,128)} %get-tuple-element.115), channel_id=1, source_target_pairs={{0,16},{1,17},{2,18},{3,19},{8,24},{9,25},{10,26},{11,27},{16,0},{... | collective-permute-start | bytes 2002952 | tf_op jit(solution)/shard_map/ppermute | solution.py:428
  141.0 9.6 %shard_map.52.refs_0_ = f32[24,24,384]{2,1,0:T(8,128)} custom-call(f32[2,24,8,384]{3,2,1,0:T(8,128)} %bitcast.14, f32[24,24,8,384]{3,2,1,0:T(8,128)} %get-tuple-element.63.rows_ref.next_ref.prev_ref, f32[24,24,8,384]{3,2,1,0:T(8,128)} %get-tuple-element.63.rows_ref.next_ref.prev_ref, f32[2,24,2,8,384]{4,3,2,1,0:T(8,128)} %bitcast.6, ...), custom_call_target="tpu_custom_call" | custom-call | flops 100000000 | bytes 16777216 | tf_op jit(solution)/shard_map/pallas_call | solution.py:496
  150.6 0.1 collective-permute-start.9
  150.7 9.8 %shard_map.53.refs_0_ = f32[24,24,384]{2,1,0:T(8,128)} custom-call(f32[24,24,8,384]{3,2,1,0:T(8,128)} %get-tuple-element.63.rows_ref.next_ref.prev_ref, f32[24,24,8,384]{3,2,1,0:T(8,128)} %get-tuple-element.63.rows_ref.next_ref.prev_ref, f32[24,24,8,384]{3,2,1,0:T(8,128)} %get-tuple-element.63.rows_ref.next_ref.prev_ref, ...), custom_call_target="tpu_custom_call", output_to_operand_aliasing={{}: (7, {})} | custom-call | flops 100000000 | bytes 16777216 | tf_op jit(solution)/shard_map/pallas_call | solution.py:496
  160.5 21.0 %collective-permute-done.12.refs_5_ = f32[8,20864]{1,0:T(8,128)S(1)} collective-permute-done((f32[8,20864]{1,0:T(8,128)}, f32[8,20864]{1,0:T(8,128)S(1)}, u32[]{:S(2)}, u32[]{:S(2)}) %collective-permute-start.12) | collective-permute-done | bytes 667680 | tf_op jit(solution)/shard_map/ppermute | solution.py:428
  181.5 0.0 collective-permute-start.13
  181.5 0.0 collective-permute-done.18.refs_6_
  181.5 14.4 %collective-permute-start.21 = (f32[8,20864]{1,0:T(8,128)}, f32[8,20864]{1,0:T(8,128)S(1)}, u32[]{:S(2)}, u32[]{:S(2)}) collective-permute-start(f32[8,20864]{1,0:T(8,128)} %get-tuple-element.119), channel_id=1, source_target_pairs={{0,8},{1,9},{2,10},{3,11},{8,0},{9,1},{10,2},{11,3},{16,24},{17,25... | collective-permute-start | bytes 2002952 | tf_op jit(solution)/shard_map/ppermute | solution.py:428
  195.9 0.0 collective-permute-done.19.refs_8_
  195.9 1.5 collective-permute-start.22
  197.4 9.6 %shard_map.54 = f32[24,24,384]{2,1,0:T(8,128)} custom-call(f32[24,24,8,384]{3,2,1,0:T(8,128)} %get-tuple-element.63.rows_ref.next_ref.prev_ref, f32[24,24,8,384]{3,2,1,0:T(8,128)} %get-tuple-element.63.rows_ref.next_ref.prev_ref, f32[2,24,8,384]{3,2,1,0:T(8,128)} %bitcast.13, f32[2,24,2,8,384]{4,3,2,1,0:T(8,128)} %bitcast.10, ...), custom_call_target="tpu_custom_call", output_to_operand_aliasing={{}: (7, {})} | custom-call | flops 100000000 | bytes 16777216 | tf_op jit(solution)/shard_map/pallas_call | solution.py:496
  207.1 0.1 collective-permute-start.10
  207.2 2.9 %shard_map.55 = (f32[16,8,20736]{2,1,0:T(8,128)}, s32[3]{0:T(128)}) custom-call(f32[8,13952]{1,0:T(8,128)} %copy-done.15, f32[8,13952]{1,0:T(8,128)} %copy-done.16, f32[8,13952]{1,0:T(8,128)} %collective-permute-done.7.refs_2_), custom_call_target="tpu_custom_call" | custom-call | tf_op jit(solution)/shard_map/pallas_call | solution.py:278
  210.1 19.8 %collective-permute-done.10.refs_0_ = f32[8,6912]{1,0:T(8,128)S(1)} collective-permute-done((f32[8,6912]{1,0:T(8,128)}, f32[8,6912]{1,0:T(8,128)S(1)}, u32[]{:S(2)}, u32[]{:S(2)}) %collective-permute-start.10) | collective-permute-done | bytes 221216 | tf_op jit(solution)/shard_map/ppermute | solution.py:428
  229.9 3.3 %collective-permute-start.15 = (f32[8,6912]{1,0:T(8,128)}, f32[8,6912]{1,0:T(8,128)S(1)}, u32[]{:S(2)}, u32[]{:S(2)}) collective-permute-start(f32[8,6912]{1,0:T(8,128)} %get-tuple-element.106), channel_id=1, source_target_pairs={{0,27},{1,26},{2,25},{3,24},{8,19},{9,18},{10,17},{11,16},{16,11},... | collective-permute-start | bytes 663560 | tf_op jit(solution)/shard_map/ppermute | solution.py:428
  233.2 3.1 %collective-permute-start.14 = (f32[8,6912]{1,0:T(8,128)}, f32[8,6912]{1,0:T(8,128)S(1)}, u32[]{:S(2)}, u32[]{:S(2)}) collective-permute-start(f32[8,6912]{1,0:T(8,128)} %get-tuple-element.104), channel_id=1, source_target_pairs={{0,2},{1,3},{2,0},{3,1},{8,10},{9,11},{10,8},{11,9},{16,18},{17,19... | collective-permute-start | bytes 663560 | tf_op jit(solution)/shard_map/ppermute | solution.py:428
  236.4 0.8 copy-done.12
  237.2 7.3 %shard_map.57 = (f32[16,8,20736]{2,1,0:T(8,128)}, s32[13]{0:T(128)}) custom-call(f32[8,20864]{1,0:T(8,128)} %get-tuple-element.107.refs_0_, f32[8,20864]{1,0:T(8,128)} %copy-done.4, f32[8,20864]{1,0:T(8,128)} %copy-done.5, f32[8,20864]{1,0:T(8,128)} %copy-done.6, f32[8,20864]{1,0:T(8,128)} %copy-done.9, ...), custom_call_target="tpu_custom_call", output_to_operand_aliasing={{0}: (13, {})} | custom-call | tf_op jit(solution)/shard_map/pallas_call | solution.py:278
  244.5 7.8 %collective-permute-done.14.refs_1_ = f32[8,6912]{1,0:T(8,128)S(1)} collective-permute-done((f32[8,6912]{1,0:T(8,128)}, f32[8,6912]{1,0:T(8,128)S(1)}, u32[]{:S(2)}, u32[]{:S(2)}) %collective-permute-start.14) | collective-permute-done | bytes 221216 | tf_op jit(solution)/shard_map/ppermute | solution.py:428
  252.3 1.4 shard_map.58
  (44 shorter events, 0.1 us)
Async XLA Ops:
  0.6 33.5 %copy-start.17 = (s32[1,1,16]{2,1,0:T(1,128)S(1)}, s32[1,1,16]{2,1,0:T(1,128)}, u32[]{:S(2)}) copy-start(s32[1,1,16]{2,1,0:T(1,128)} %owner_ref.1) | copy-start | bytes 196
  11.7 20.4 %collective-permute-start.1 = (f32[2,48,8,384]{3,2,1,0:T(8,128)}, f32[2,48,8,384]{3,2,1,0:T(8,128)S(1)}, u32[]{:S(2)}, u32[]{:S(2)}) collective-permute-start(f32[2,48,8,384]{3,2,1,0:T(8,128)} %get-tuple-element.65), channel_id=1, source_target_pairs={{0,4},{4,0},{1,5},{5,1},{2,6},{6,2},{3,7},{7,3},{8,12},{12,8},{9,1... | collective-permute-start | bytes 3538952 | tf_op jit(solution)/shard_map/ppermute | solution.py:428
  12.2 17.9 %collective-permute-start.2 = (f32[48,8,384]{2,1,0:T(8,128)}, f32[48,8,384]{2,1,0:T(8,128)S(1)}, u32[]{:S(2)}, u32[]{:S(2)}) collective-permute-start(f32[48,8,384]{2,1,0:T(8,128)} %get-tuple-element.67), channel_id=1, source_target_pairs={{0,8},{8,16},{16,24},{24,0},{1,9},{9,17},{17,25},{25,1},{2,10},{10... | collective-permute-start | bytes 1769480 | tf_op jit(solution)/shard_map/ppermute | solution.py:428
  14.7 37.6 %collective-permute-start = (f32[48,8,384]{2,1,0:T(8,128)}, f32[48,8,384]{2,1,0:T(8,128)S(1)}, u32[]{:S(2)}, u32[]{:S(2)}) collective-permute-start(f32[48,8,384]{2,1,0:T(8,128)} %get-tuple-element.64), channel_id=1, source_target_pairs={{0,24},{8,0},{16,8},{24,16},{1,25},{9,1},{17,9},{25,17},{2,26},{10... | collective-permute-start | bytes 1769480 | tf_op jit(solution)/shard_map/ppermute | solution.py:428
  15.8 18.9 %collective-permute-start.5 = (f32[8,13952]{1,0:T(8,128)}, f32[8,13952]{1,0:T(8,128)S(1)}, u32[]{:S(2)}, u32[]{:S(2)}) collective-permute-start(f32[8,13952]{1,0:T(8,128)} %get-tuple-element.71), channel_id=1, source_target_pairs={{0,3},{1,2},{2,1},{3,0},{8,11},{9,10},{10,9},{11,8},{16,19},{17,18... | collective-permute-start | bytes 1339400 | tf_op jit(solution)/shard_map/ppermute | solution.py:428
  19.8 49.7 %collective-permute-start.6 = (f32[8,13952]{1,0:T(8,128)}, f32[8,13952]{1,0:T(8,128)S(1)}, u32[]{:S(2)}, u32[]{:S(2)}) collective-permute-start(f32[8,13952]{1,0:T(8,128)} %get-tuple-element.72), channel_id=1, source_target_pairs={{0,2},{1,3},{2,0},{3,1},{8,10},{9,11},{10,8},{11,9},{16,18},{17,19... | collective-permute-start | bytes 1339400 | tf_op jit(solution)/shard_map/ppermute | solution.py:428
  30.1 22.2 %copy-start.3 = (f32[48,8,384]{2,1,0:T(8,128)}, f32[48,8,384]{2,1,0:T(8,128)S(1)}, u32[]{:S(2)}) copy-start(f32[48,8,384]{2,1,0:T(8,128)S(1)} %collective-permute-done.2.x_low) | copy-start | bytes 1769476
  30.1 22.2 %collective-permute-start.3 = (f32[8,1152]{1,0:T(8,128)}, f32[8,1152]{1,0:T(8,128)S(1)}, u32[]{:S(2)}, u32[]{:S(2)}) collective-permute-start(f32[8,1152]{1,0:T(8,128)} %get-tuple-element.68), channel_id=1, source_target_pairs={{0,1},{1,2},{2,3},{3,0},{4,5},{5,6},{6,7},{7,4},{8,9},{9,10},{10,1... | collective-permute-start | bytes 110600 | tf_op jit(solution)/shard_map/ppermute | solution.py:428
  32.1 20.3 %copy-start.1 = (f32[2,48,8,384]{3,2,1,0:T(8,128)}, f32[2,48,8,384]{3,2,1,0:T(8,128)S(1)}, u32[]{:S(2)}) copy-start(f32[2,48,8,384]{3,2,1,0:T(8,128)S(1)} %collective-permute-done.1.y_halos) | copy-start | bytes 3538948
  32.1 20.2 %collective-permute-start.4 = (f32[8,1152]{1,0:T(8,128)}, f32[8,1152]{1,0:T(8,128)S(1)}, u32[]{:S(2)}, u32[]{:S(2)}) collective-permute-start(f32[8,1152]{1,0:T(8,128)} %get-tuple-element.70), channel_id=1, source_target_pairs={{0,3},{1,0},{2,1},{3,2},{4,7},{5,4},{6,5},{7,6},{8,11},{9,8},{10,9... | collective-permute-start | bytes 110600 | tf_op jit(solution)/shard_map/ppermute | solution.py:428
  34.7 45.7 %copy-start.15 = (f32[8,13952]{1,0:T(8,128)}, f32[8,13952]{1,0:T(8,128)S(1)}, u32[]{:S(2)}) copy-start(f32[8,13952]{1,0:T(8,128)S(1)} %collective-permute-done.5.refs_0_) | copy-start | bytes 1339396
  34.7 45.7 %collective-permute-start.7 = (f32[8,13952]{1,0:T(8,128)}, f32[8,13952]{1,0:T(8,128)}, u32[]{:S(2)}, u32[]{:S(2)}) collective-permute-start(f32[8,13952]{1,0:T(8,128)} %get-tuple-element.74), channel_id=1, source_target_pairs={{0,27},{1,26},{2,25},{3,24},{8,19},{9,18},{10,17},{11,16},{16,11},... | collective-permute-start | bytes 1339400 | tf_op jit(solution)/shard_map/ppermute | solution.py:428
  52.3 0.8 copy-start.2
  52.3 0.8 copy-start.13
  52.3 0.8 copy-start.14
  69.5 11.0 %copy-start.16 = (f32[8,13952]{1,0:T(8,128)}, f32[8,13952]{1,0:T(8,128)S(1)}, u32[]{:S(2)}) copy-start(f32[8,13952]{1,0:T(8,128)S(1)} %collective-permute-done.6.refs_1_) | copy-start | bytes 1339396
  69.5 42.9 %collective-permute-start.11 = (f32[8,20864]{1,0:T(8,128)}, f32[8,20864]{1,0:T(8,128)S(1)}, u32[]{:S(2)}, u32[]{:S(2)}) collective-permute-start(f32[8,20864]{1,0:T(8,128)} %get-tuple-element.101), channel_id=1, source_target_pairs={{0,26},{1,27},{2,24},{3,25},{8,18},{9,19},{10,16},{11,17},{16,10},... | collective-permute-start | bytes 2002952 | tf_op jit(solution)/shard_map/ppermute | solution.py:428
  80.4 54.3 %collective-permute-start.16 = (f32[8,20864]{1,0:T(8,128)}, f32[8,20864]{1,0:T(8,128)S(1)}, u32[]{:S(2)}, u32[]{:S(2)}) collective-permute-start(f32[8,20864]{1,0:T(8,128)} %get-tuple-element.109), channel_id=1, source_target_pairs={{0,25},{1,24},{2,27},{3,26},{8,17},{9,16},{10,19},{11,18},{16,9},{... | collective-permute-start | bytes 2002952 | tf_op jit(solution)/shard_map/ppermute | solution.py:428
  80.5 70.2 %collective-permute-start.8 = (f32[8,20864]{1,0:T(8,128)}, f32[8,20864]{1,0:T(8,128)S(1)}, u32[]{:S(2)}, u32[]{:S(2)}) collective-permute-start(f32[8,20864]{1,0:T(8,128)} %get-tuple-element.94), channel_id=1, source_target_pairs={{0,11},{1,10},{2,9},{3,8},{8,3},{9,2},{10,1},{11,0},{16,27},{17,26... | collective-permute-start | bytes 2002952 | tf_op jit(solution)/shard_map/ppermute | solution.py:428
  112.3 38.3 %copy-start.4 = (f32[8,20864]{1,0:T(8,128)}, f32[8,20864]{1,0:T(8,128)S(1)}, u32[]{:S(2)}) copy-start(f32[8,20864]{1,0:T(8,128)S(1)} %collective-permute-done.11.refs_1_) | copy-start | bytes 2002948
  112.3 69.2 %collective-permute-start.12 = (f32[8,20864]{1,0:T(8,128)}, f32[8,20864]{1,0:T(8,128)S(1)}, u32[]{:S(2)}, u32[]{:S(2)}) collective-permute-start(f32[8,20864]{1,0:T(8,128)} %get-tuple-element.102), channel_id=1, source_target_pairs={{0,10},{1,11},{2,8},{3,9},{8,2},{9,3},{10,0},{11,1},{16,26},{17,27... | collective-permute-start | bytes 2002952 | tf_op jit(solution)/shard_map/ppermute | solution.py:428
  112.3 69.2 %collective-permute-start.18 = (f32[8,20864]{1,0:T(8,128)}, f32[8,20864]{1,0:T(8,128)S(1)}, u32[]{:S(2)}, u32[]{:S(2)}) collective-permute-start(f32[8,20864]{1,0:T(8,128)} %get-tuple-element.113), channel_id=1, source_target_pairs={{0,17},{1,16},{2,19},{3,18},{8,25},{9,24},{10,27},{11,26},{16,1},{... | collective-permute-start | bytes 2002952 | tf_op jit(solution)/shard_map/ppermute | solution.py:428
  134.8 61.1 %collective-permute-start.17 = (f32[8,20864]{1,0:T(8,128)}, f32[8,20864]{1,0:T(8,128)S(1)}, u32[]{:S(2)}, u32[]{:S(2)}) collective-permute-start(f32[8,20864]{1,0:T(8,128)} %get-tuple-element.111), channel_id=1, source_target_pairs={{0,24},{1,25},{2,26},{3,27},{8,16},{9,17},{10,18},{11,19},{16,8},{... | collective-permute-start | bytes 2002952 | tf_op jit(solution)/shard_map/ppermute | solution.py:428
  134.8 15.8 %copy-start.5 = (f32[8,20864]{1,0:T(8,128)}, f32[8,20864]{1,0:T(8,128)S(1)}, u32[]{:S(2)}) copy-start(f32[8,20864]{1,0:T(8,128)S(1)} %collective-permute-done.16.refs_2_) | copy-start | bytes 2002948
  134.8 61.1 %collective-permute-start.19 = (f32[8,20864]{1,0:T(8,128)}, f32[8,20864]{1,0:T(8,128)}, u32[]{:S(2)}, u32[]{:S(2)}) collective-permute-start(f32[8,20864]{1,0:T(8,128)} %get-tuple-element.115), channel_id=1, source_target_pairs={{0,16},{1,17},{2,18},{3,19},{8,24},{9,25},{10,26},{11,27},{16,0},{... | collective-permute-start | bytes 2002952 | tf_op jit(solution)/shard_map/ppermute | solution.py:428
  150.6 9.9 %copy-start.6 = (f32[8,20864]{1,0:T(8,128)}, f32[8,20864]{1,0:T(8,128)S(1)}, u32[]{:S(2)}) copy-start(f32[8,20864]{1,0:T(8,128)S(1)} %collective-permute-done.8.refs_3_) | copy-start | bytes 2002948
  150.6 56.4 %collective-permute-start.9 = (f32[8,20864]{1,0:T(8,128)}, f32[8,20864]{1,0:T(8,128)S(1)}, u32[]{:S(2)}, u32[]{:S(2)}) collective-permute-start(f32[8,20864]{1,0:T(8,128)} %get-tuple-element.95), channel_id=1, source_target_pairs={{0,19},{1,18},{2,17},{3,16},{8,27},{9,26},{10,25},{11,24},{16,3},{... | collective-permute-start | bytes 2002952 | tf_op jit(solution)/shard_map/ppermute | solution.py:428
  181.5 25.6 %copy-start.7 = (f32[8,20864]{1,0:T(8,128)}, f32[8,20864]{1,0:T(8,128)S(1)}, u32[]{:S(2)}) copy-start(f32[8,20864]{1,0:T(8,128)S(1)} %collective-permute-done.12.refs_5_) | copy-start | bytes 2002948
  181.5 51.7 %collective-permute-start.13 = (f32[8,20864]{1,0:T(8,128)}, f32[8,20864]{1,0:T(8,128)S(1)}, u32[]{:S(2)}, u32[]{:S(2)}) collective-permute-start(f32[8,20864]{1,0:T(8,128)} %get-tuple-element.103), channel_id=1, source_target_pairs={{0,18},{1,19},{2,16},{3,17},{8,26},{9,27},{10,24},{11,25},{16,2},{... | collective-permute-start | bytes 2002952 | tf_op jit(solution)/shard_map/ppermute | solution.py:428
  181.5 25.6 %copy-start.8 = (f32[8,20864]{1,0:T(8,128)}, f32[8,20864]{1,0:T(8,128)S(1)}, u32[]{:S(2)}) copy-start(f32[8,20864]{1,0:T(8,128)S(1)} %collective-permute-done.18.refs_6_) | copy-start | bytes 2002948
  181.5 54.8 %collective-permute-start.21 = (f32[8,20864]{1,0:T(8,128)}, f32[8,20864]{1,0:T(8,128)S(1)}, u32[]{:S(2)}, u32[]{:S(2)}) collective-permute-start(f32[8,20864]{1,0:T(8,128)} %get-tuple-element.119), channel_id=1, source_target_pairs={{0,8},{1,9},{2,10},{3,11},{8,0},{9,1},{10,2},{11,3},{16,24},{17,25... | collective-permute-start | bytes 2002952 | tf_op jit(solution)/shard_map/ppermute | solution.py:428
  195.9 11.2 %copy-start.9 = (f32[8,20864]{1,0:T(8,128)}, f32[8,20864]{1,0:T(8,128)S(1)}, u32[]{:S(2)}) copy-start(f32[8,20864]{1,0:T(8,128)S(1)} %collective-permute-done.17.refs_4_) | copy-start | bytes 2002948
  195.9 40.5 %collective-permute-start.20 = (f32[8,20864]{1,0:T(8,128)}, f32[8,20864]{1,0:T(8,128)}, u32[]{:S(2)}, u32[]{:S(2)}) collective-permute-start(f32[8,20864]{1,0:T(8,128)} %get-tuple-element.117), channel_id=1, source_target_pairs={{0,9},{1,8},{2,11},{3,10},{8,1},{9,0},{10,3},{11,2},{16,25},{17,24... | collective-permute-start | bytes 2002952 | tf_op jit(solution)/shard_map/ppermute | solution.py:428
  195.9 40.5 %collective-permute-start.22 = (f32[8,20864]{1,0:T(8,128)}, f32[8,20864]{1,0:T(8,128)}, u32[]{:S(2)}, u32[]{:S(2)}) collective-permute-start(f32[8,20864]{1,0:T(8,128)} %get-tuple-element.121), channel_id=1, source_target_pairs={{0,1},{1,0},{2,3},{3,2},{8,9},{9,8},{10,11},{11,10},{16,17},{17,16... | collective-permute-start | bytes 2002952 | tf_op jit(solution)/shard_map/ppermute | solution.py:428
  207.1 29.3 %copy-start.10 = (f32[8,20864]{1,0:T(8,128)}, f32[8,20864]{1,0:T(8,128)S(1)}, u32[]{:S(2)}) copy-start(f32[8,20864]{1,0:T(8,128)S(1)} %collective-permute-done.9.refs_7_) | copy-start | bytes 2002948
  207.1 22.8 %collective-permute-start.10 = (f32[8,6912]{1,0:T(8,128)}, f32[8,6912]{1,0:T(8,128)S(1)}, u32[]{:S(2)}, u32[]{:S(2)}) collective-permute-start(f32[8,6912]{1,0:T(8,128)} %get-tuple-element.96), channel_id=1, source_target_pairs={{0,3},{1,2},{2,1},{3,0},{8,11},{9,10},{10,9},{11,8},{16,19},{17,18... | collective-permute-start | bytes 663560 | tf_op jit(solution)/shard_map/ppermute | solution.py:428
  229.9 14.6 %collective-permute-start.15 = (f32[8,6912]{1,0:T(8,128)}, f32[8,6912]{1,0:T(8,128)S(1)}, u32[]{:S(2)}, u32[]{:S(2)}) collective-permute-start(f32[8,6912]{1,0:T(8,128)} %get-tuple-element.106), channel_id=1, source_target_pairs={{0,27},{1,26},{2,25},{3,24},{8,19},{9,18},{10,17},{11,16},{16,11},... | collective-permute-start | bytes 663560 | tf_op jit(solution)/shard_map/ppermute | solution.py:428
  233.2 3.2 %copy-start.11 = (f32[8,20864]{1,0:T(8,128)}, f32[8,20864]{1,0:T(8,128)S(1)}, u32[]{:S(2)}) copy-start(f32[8,20864]{1,0:T(8,128)S(1)} %collective-permute-done.13.refs_9_) | copy-start | bytes 2002948
  233.2 19.1 %collective-permute-start.14 = (f32[8,6912]{1,0:T(8,128)}, f32[8,6912]{1,0:T(8,128)S(1)}, u32[]{:S(2)}, u32[]{:S(2)}) collective-permute-start(f32[8,6912]{1,0:T(8,128)} %get-tuple-element.104), channel_id=1, source_target_pairs={{0,2},{1,3},{2,0},{3,1},{8,10},{9,11},{10,8},{11,9},{16,18},{17,19... | collective-permute-start | bytes 663560 | tf_op jit(solution)/shard_map/ppermute | solution.py:428
  236.4 0.8 copy-start.12
  237.2 15.1 %copy-start = (s32[3]{0:T(128)S(1)}, s32[3]{0:T(128)}, u32[]{:S(2)}) copy-start(s32[3]{0:T(128)} %get-tuple-element.75.slots_ref) | copy-start | bytes 40
